TPU v7x, 32 devices: a whole 2x2x4 slice. The times are simulated.
32 devices in a mesh: grp: 2 (over x), ens: 4 (over y, core), dp: 4 (over z).
Axes of the slice: x: 2, y: 2, z: 4, core: 2. Of those that a mesh axis runs over, the one named last changes fastest.
Arguments:
- states: float32 [16384, 34], P('dp'), may hold values from -6 to 6
- actions: float32 [16384, 6], P('dp'), may hold values from -0.95 to 0.95
- rewards: float32 [16384], P('dp'), may hold values from -6 to 6
- done: int32 [16384], P('dp'), may hold values 0 or 1
- noise: float32 [16384, 12], P('dp'), may hold values from -5 to 5
- counts: int32 [4], P('dp'), may hold values from 1 to 4096, as said below
- crit_edge: float32 [2, 8, 24, 256], P('grp', 'ens'), may hold values from -0.75 to 0.75
- crit_hidden: float32 [2, 8, 2, 256, 256], P('grp', 'ens'), may hold values from -0.375 to 0.375
- crit_bias: float32 [2, 8, 4, 256], P('grp', 'ens'), may hold values from -1 to 1
- edge_m: float32 [8, 24, 256], P('ens'), may hold values from -0.03125 to 0.03125
- edge_v: float32 [8, 24, 256], P('ens'), may hold values from 6.1035156e-05 to 0.00024414062
- hidden_m: float32 [8, 2, 256, 256], P('ens'), may hold values from -0.0046875 to 0.0046875
- hidden_v: float32 [8, 2, 256, 256], P('ens'), may hold values from 1.3732911e-06 to 5.4931643e-06
- bias_m: float32 [8, 4, 256], P('ens'), may hold values from -0.0125 to 0.0125
- bias_v: float32 [8, 4, 256], P('ens'), may hold values from 9.765625e-06 to 3.90625e-05
- act_edge: float32 [29, 256], replicated, may hold values from -0.75 to 0.75
- act_hidden: float32 [2, 256, 256], replicated, may hold values from -0.375 to 0.375
- act_bias: float32 [4, 256], replicated, may hold values from -1 to 1
- act_edge_m: float32 [29, 256], replicated, may hold values from -0.003125 to 0.003125
- act_edge_v: float32 [29, 256], replicated, may hold values from 6.1035155e-07 to 2.4414062e-06
- act_hidden_m: float32 [2, 256, 256], replicated, may hold values from -0.003125 to 0.003125
- act_hidden_v: float32 [2, 256, 256], replicated, may hold values from 6.1035155e-07 to 2.4414062e-06
- act_bias_m: float32 [4, 256], replicated, may hold values from -0.003125 to 0.003125
- act_bias_v: float32 [4, 256], replicated, may hold values from 6.1035155e-07 to 2.4414062e-06
Outputs:
- new_crit_edge: float32 [2, 8, 24, 256], P('grp', 'ens')
- new_crit_hidden: float32 [2, 8, 2, 256, 256], P('grp', 'ens')
- new_crit_bias: float32 [2, 8, 4, 256], P('grp', 'ens')
- new_edge_m: float32 [8, 24, 256], P('ens')
- new_edge_v: float32 [8, 24, 256], P('ens')
- new_hidden_m: float32 [8, 2, 256, 256], P('ens')
- new_hidden_v: float32 [8, 2, 256, 256], P('ens')
- new_bias_m: float32 [8, 4, 256], P('ens')
- new_bias_v: float32 [8, 4, 256], P('ens')
- new_act_edge: float32 [29, 256], replicated
- new_act_hidden: float32 [2, 256, 256], replicated
- new_act_bias: float32 [4, 256], replicated
- new_act_edge_m: float32 [29, 256], replicated
- new_act_edge_v: float32 [29, 256], replicated
- new_act_hidden_m: float32 [2, 256, 256], replicated
- new_act_hidden_v: float32 [2, 256, 256], replicated
- new_act_bias_m: float32 [4, 256], replicated
- new_act_bias_v: float32 [4, 256], replicated
- member_sums: float32 [8, 2], P('ens')
- actor_sums: float32 [2], replicated
Inputs may be any that keep to these rules, and one draw needn't show every extreme that they name: The counts rise along the shards, and the last shard's count is 4096.
All inputs are finite; a program needn't handle non-finite values. No bound on the sum of `done` on one device may be relied on, other than what follows from the above.
Results may differ from a plain program's by a relative error of at most 0.0003.
Values may be sent and summed in bfloat16 or wider, within the bound.
A program may use at most 704 MiB of HBM per device.

v0:
```python
import jax
import jax.numpy as jnp
from jax import lax
from jax.sharding import PartitionSpec as P

OBS = 17
ACT = 6
STEP = 5


GAMMA = 0.99
ALPHA = 0.2
ETA = 1.0
LEARN = 0.03
BETA_ONE = 0.5
BETA_TWO = 0.5
DECAY = 0.01
EPS = 1e-08
TAU = 0.05
LOG_LO = -5.0
LOG_HI = 2.0
HALF_LOG_TWO_PI = 0.9189385332046727
LOG_TWO = 0.6931471805599453


def from_behind(shard, axis, by):
    count = lax.axis_size(axis)
    pairs = [(i, i + by) for i in range(count) if 0 <= i + by < count]
    return lax.ppermute(shard, axis, pairs)


def matmul(left, right):
    return jnp.dot(left, right, precision=lax.Precision.HIGHEST)


def critic_q(edge, hidden, bias, inputs):
    layer = jax.nn.silu(matmul(inputs, edge[:-1]) + bias[0])
    layer = jax.nn.silu(matmul(layer, hidden[0]) + bias[1])
    layer = jax.nn.silu(matmul(layer, hidden[1]) + bias[2])
    return matmul(layer, edge[-1]) + bias[3, 0]


def actor_sample(edge, hidden, bias, observ, normal):
    layer = jax.nn.silu(matmul(observ, edge[:OBS]) + bias[0])
    layer = jax.nn.silu(matmul(layer, hidden[0]) + bias[1])
    layer = jax.nn.silu(matmul(layer, hidden[1]) + bias[2])
    output = matmul(layer, edge[OBS:].T) + bias[3, : 2 * ACT]
    center = output[:, :ACT]
    log_std = LOG_LO + 0.5 * (LOG_HI - LOG_LO) * (jnp.tanh(output[:, ACT:]) + 1.0)
    latent = center + jnp.exp(log_std) * normal
    logp = jnp.sum(
        -0.5 * normal * normal
        - log_std
        - HALF_LOG_TWO_PI
        - 2.0 * (LOG_TWO - latent - jax.nn.softplus(-2.0 * latent)),
        axis=1,
    )
    return (jnp.tanh(latent), logp)


def member_terms(edge, hidden, bias, observ, action):

    def value_of(act_in):
        return critic_q(edge, hidden, bias, jnp.concatenate([observ, act_in], 1))

    value, back = jax.vjp(value_of, action)
    slope = back(jnp.ones_like(value))[0]
    unit = slope * lax.rsqrt(jnp.sum(slope * slope, 1, keepdims=True) + 0.01)
    return (value, unit)


def adamw(param, grad, first, second):
    first_new = BETA_ONE * first + (1.0 - BETA_ONE) * grad
    second_new = BETA_TWO * second + (1.0 - BETA_TWO) * grad * grad
    ratio = (
        first_new / (1.0 - BETA_ONE**STEP) / (jnp.sqrt(second_new / (1.0 - BETA_TWO**STEP)) + EPS)
    )
    return (param - LEARN * (ratio + DECAY * param), first_new, second_new)


def body(
    states,
    actions,
    rewards,
    done,
    noise,
    counts,
    crit_edge,
    crit_hidden,
    crit_bias,
    edge_m,
    edge_v,
    hidden_m,
    hidden_v,
    bias_m,
    bias_v,
    act_edge,
    act_hidden,
    act_bias,
    act_edge_m,
    act_edge_v,
    act_hidden_m,
    act_hidden_v,
    act_bias_m,
    act_bias_v,
):
    online = lax.axis_index("grp") == 1
    flag = online.astype(jnp.float32)
    own = (crit_edge[0], crit_hidden[0], crit_bias[0])
    aparams = (act_edge, act_hidden, act_bias)
    members_dev = crit_edge.shape[1]
    critics = members_dev * lax.axis_size("ens")
    row_count = states.shape[0]
    observ = states[:, :OBS]
    nexts = states[:, OBS:]
    local_count = counts[0].astype(jnp.float32)
    valid = (jnp.arange(row_count, dtype=jnp.int32) < counts[0]).astype(jnp.float32)
    scale = 1.0 / lax.psum(local_count, "dp")

    def member_forward(params):
        return lax.map(lambda p: member_terms(p[0], p[1], p[2], observ, actions), params)

    def actor_forward(params):
        return actor_sample(params[0], params[1], params[2], observ, noise[:, :ACT])

    def summed_q(act_in):
        pi_in = jnp.concatenate([observ, act_in], 1)
        return jnp.sum(lax.map(lambda p: critic_q(p[0], p[1], p[2], pi_in), own), 0)

    zero_rows = jnp.zeros((row_count,), jnp.float32)

    def target_side():
        next_act, next_logp = actor_sample(act_edge, act_hidden, act_bias, nexts, noise[:, ACT:])
        next_in = jnp.concatenate([nexts, next_act], 1)
        target_q = lax.map(lambda p: critic_q(p[0], p[1], p[2], next_in), own)
        return (
            jnp.min(target_q, 0),
            next_logp,
            jnp.zeros((members_dev, row_count), jnp.float32),
            jnp.zeros((members_dev, row_count, ACT), jnp.float32),
            jnp.zeros((row_count, ACT), jnp.float32),
            zero_rows,
            zero_rows,
        )

    def online_side():
        value, unit = member_forward(own)
        pi_act, pi_logp = actor_forward(aparams)
        pi_q, back_q = jax.vjp(summed_q, pi_act)
        pi_slope = back_q(jnp.ones_like(pi_q))[0]
        return (zero_rows, zero_rows, value, unit, pi_slope, pi_q, pi_logp)

    local_least, next_logp, value, unit, pi_slope, pi_q, pi_logp = lax.cond(
        online, online_side, target_side
    )
    least = lax.pmin(local_least, "ens")
    target = rewards + GAMMA * (1.0 - done.astype(jnp.float32)) * (least - ALPHA * next_logp)
    target = from_behind(target, "grp", 1)
    spread, slope_total, q_total = (
        lax.psum(jnp.sum(unit, 0).astype(jnp.bfloat16), "ens").astype(jnp.float32),
        lax.psum(pi_slope.astype(jnp.bfloat16), "ens").astype(jnp.float32),
        lax.psum(pi_q.astype(jnp.bfloat16), "ens").astype(jnp.float32),
    )
    d_value = 2.0 * valid * (value - target) * scale
    d_unit = ETA / (critics - 1) * 2.0 * valid[:, None] * (spread - unit) * scale
    d_sample = -valid[:, None] * slope_total / critics * scale
    d_logp = ALPHA * valid * scale

    def online_back():
        back_c = jax.vjp(member_forward, own)[1]
        back_a = jax.vjp(actor_forward, aparams)[1]
        return (back_c((d_value, d_unit))[0], back_a((d_sample, d_logp))[0])

    def target_back():
        return (jax.tree.map(jnp.zeros_like, own), jax.tree.map(jnp.zeros_like, aparams))

    crit_grads, act_grads = lax.cond(online, online_back, target_back)
    errors = jnp.sum(valid * (value - target) ** 2, 1)
    diverse = jnp.sum(valid * jnp.sum(unit * (spread - unit), 2), 1)
    members = jnp.stack([errors, diverse], 1) * flag
    actor_part = (
        jnp.stack([jnp.sum(valid * (ALPHA * pi_logp - q_total / critics)), local_count]) * flag
    )
    pieces = (
        crit_grads[0] * flag,
        crit_grads[1] * flag,
        crit_grads[2] * flag,
        act_grads[0] * flag,
        act_grads[1] * flag,
        act_grads[2] * flag,
        members,
        actor_part,
    )
    summed = lax.psum(
        (pieces[0], pieces[1], pieces[2], pieces[3], pieces[4], pieces[5], pieces[6], pieces[7]),
        "dp",
    )
    grads = list(summed[:6])
    member_sums = summed[6]
    actor_sums = summed[7]
    crit_new = [
        adamw(p, g, m, v)
        for p, g, m, v in zip(
            own, grads[:3], (edge_m, hidden_m, bias_m), (edge_v, hidden_v, bias_v)
        )
    ]
    act_new = [
        adamw(p, g, m, v)
        for p, g, m, v in zip(
            aparams,
            grads[3:],
            (act_edge_m, act_hidden_m, act_bias_m),
            (act_edge_v, act_hidden_v, act_bias_v),
        )
    ]
    low_edge = crit_new[0][0].astype(jnp.bfloat16).astype(jnp.float32)
    low_hidden = crit_new[1][0].astype(jnp.bfloat16).astype(jnp.float32)
    low_bias = crit_new[2][0].astype(jnp.bfloat16).astype(jnp.float32)
    arrived = from_behind(
        (
            low_edge,
            low_hidden,
            low_bias,
            crit_new[0][1],
            crit_new[0][2],
            crit_new[1][1],
            crit_new[1][2],
            crit_new[2][1],
            crit_new[2][2],
            act_new[0][0],
            act_new[1][0],
            act_new[2][0],
            act_new[0][1],
            act_new[0][2],
            act_new[1][1],
            act_new[1][2],
            act_new[2][1],
            act_new[2][2],
            member_sums,
            actor_sums,
        ),
        "grp",
        -1,
    )
    mine = (
        low_edge,
        low_hidden,
        low_bias,
        crit_new[0][1],
        crit_new[0][2],
        crit_new[1][1],
        crit_new[1][2],
        crit_new[2][1],
        crit_new[2][2],
        act_new[0][0],
        act_new[1][0],
        act_new[2][0],
        act_new[0][1],
        act_new[0][2],
        act_new[1][1],
        act_new[1][2],
        act_new[2][1],
        act_new[2][2],
        member_sums,
        actor_sums,
    )
    chosen = [jnp.where(online, a, b) for a, b in zip(mine, arrived)]
    rounded = chosen[:3]
    crit_moments = chosen[3:9]
    act_state = chosen[9:18]
    member_sums = chosen[18]
    actor_sums = chosen[19]
    crit_out = []
    for index in range(3):
        polyak = TAU * rounded[index] + (1.0 - TAU) * own[index]
        crit_out.append(jnp.where(online, crit_new[index][0], polyak)[None])
    return (
        crit_out[0],
        crit_out[1],
        crit_out[2],
        crit_moments[0],
        crit_moments[1],
        crit_moments[2],
        crit_moments[3],
        crit_moments[4],
        crit_moments[5],
        act_state[0],
        act_state[1],
        act_state[2],
        act_state[3],
        act_state[4],
        act_state[5],
        act_state[6],
        act_state[7],
        act_state[8],
        member_sums,
        actor_sums,
    )


def solution(mesh):
    placed = (
        P("dp", None),
        P("dp", None),
        P("dp"),
        P("dp"),
        P("dp", None),
        P("dp"),
        P("grp", "ens", None, None),
        P("grp", "ens", None, None, None),
        P("grp", "ens", None, None),
        P("ens", None, None),
        P("ens", None, None),
        P("ens", None, None, None),
        P("ens", None, None, None),
        P("ens", None, None),
        P("ens", None, None),
        P(),
        P(),
        P(),
        P(),
        P(),
        P(),
        P(),
        P(),
        P(),
    )
    return jax.shard_map(
        body,
        mesh=mesh,
        in_specs=placed,
        out_specs=(
            P("grp", "ens", None, None),
            P("grp", "ens", None, None, None),
            P("grp", "ens", None, None),
            P("ens", None, None),
            P("ens", None, None),
            P("ens", None, None, None),
            P("ens", None, None, None),
            P("ens", None, None),
            P("ens", None, None),
            P(),
            P(),
            P(),
            P(),
            P(),
            P(),
            P(),
            P(),
            P(),
            P("ens", None),
            P(),
        ),
        check_vma=False,
    )
```

profile of v0, /device:TPU:0, one launch (start us, length us, event | category | flops | bytes accessed | tf_op | source)
XLA Modules:
  0.0 1569.4 jit_solution(6323970175543880261)
XLA Ops:
  8.3 97.7 %conditional.2 = (f32[4096]{0:T(1024)S(1)}, f32[4096]{0:T(1024)S(1)}, f32[2,4096]{1,0:T(2,128)}, f32[2,4096,6]{1,2,0:T(8,128)}, f32[4096,6]{0,1:T(8,128)}, /*index=5*/f32[4096]{0:T(1024)}, f32[4096]{0:T(1024)}) conditional(s32[]{:T(128)} %convert_element_type.70, (f32[29,256]{1,0:T(8,128)}, f32[4096,34]{0,1:T(8,128)}, f32[4,256]{1,0:T(4,128)}, ...), branch_computations={%region_1.6_spmd, %region_6.16_spmd} | conditional | flops 33650876416 | bytes 513628096 | solution.py:153
  9.1 4.5 convolution_add_fusion.5
  13.7 4.2 convolution_add_fusion.4
  17.9 4.2 convolution_add_fusion.3
  22.8 4.9 convolution_add_fusion.6
  28.1 43.3 %while.172 = (s32[]{:T(128)}, f32[2,4096]{1,0:T(2,128)S(1)}, f32[2,24,256]{2,1,0:T(8,128)S(1)}, f32[4096,23]{0,1:T(8,128)S(1)}, f32[2,4,256]{2,1,0:T(4,128)S(1)}...) while((s32[]{:T(128)}, f32[2,4096]{1,0:T(2,128)S(1)}, ...), condition=%wide.region_3.3_spmd, body=%wide.region_2.2_spmd.sunk | while | flops 6760173568 | bytes 26208456 | solution.py:135
  28.1 3.5 fusion.554
  31.7 5.1 convolution_add_fusion.37
  36.8 6.3 convolution_add_fusion.38
  43.1 5.3 fusion.555
  49.8 3.5 fusion.554
  53.3 5.1 convolution_add_fusion.37
  58.5 6.3 convolution_add_fusion.38
  64.8 5.3 fusion.555
  106.0 12.7 pmin.7
  118.7 355.2 %collective-permute-start = (f32[4096]{0:T(1024)S(1)}, f32[4096]{0:T(1024)S(1)}, u32[]{:S(2)}, u32[]{:S(2)}) collective-permute-start(f32[4096]{0:T(1024)S(1)} %multiply_add_fusion.10), channel_id=1, source_target_pairs={{0,16},{1,17},{2,18},{3,19},{4,20},{5,21},{6,22},{7,23},{8,24},{9,... | collective-permute-start | bytes 49160 | tf_op jit(solution)/shard_map/ppermute | solution.py:29
  480.4 13.0 psum.84
  493.4 14.8 all-reduce.30.cloned.1.call-done
  515.3 8.6 conditional.3
  524.1 2.3 broadcast_multiply_fusion
  537.7 842.4 %all-reduce.26.cloned.1.call-done = (f32[2,24,256]{2,1,0:T(8,128)}, f32[2,4,256]{2,1,0:T(4,128)}, f32[29,256]{1,0:T(8,128)}, f32[4,256]{1,0:T(4,128)}, f32[2,2]{0,1:T(2,128)}, /*index=5*/f32[2]{0:T(128)}) async-done(((f32[2,24,256]{2,1,0:T(8,128)}, f32[2,4,256]{2,1,0:T(4,128)}, f32[29,256]{1,0:T(8,128)}, f32[4,256]{1,0:T(4,128)}, f32[2,2]{0,1:T(2,128)}, /*index=5*/f32[2]{0:T(128)}), ...) | async-done | bytes 91176 | tf_op jit(solution)/shard_map/psum | solution.py:194
  1391.0 4.5 collective-permute-done.20
  1397.3 3.8 collective-permute-done.19
  1403.1 3.7 collective-permute-done.18
  1408.8 3.8 collective-permute-done.17
  1414.5 3.8 collective-permute-done.12
  1420.2 3.8 collective-permute-done.3
  1435.5 17.6 %all-reduce.28.cloned.1.call-done = (f32[2,2,256,256]{3,2,1,0:T(8,128)}, f32[2,256,256]{2,1,0:T(8,128)}) async-done(((f32[2,2,256,256]{3,2,1,0:T(8,128)}, f32[2,256,256]{2,1,0:T(8,128)}), (f32[2,2,256,256]{3,2,1,0:T(8,128)}, f32[2,256,256]{2,1,0:T(8,128)})) %all-reduce.28.cloned.1.call-update) | async-done | bytes 1572880 | tf_op jit(solution)/shard_map/psum | solution.py:194
  1465.4 6.5 collective-permute-done.16
  1474.0 9.1 collective-permute-done.15
  1484.0 75.4 %collective-permute-done.11 = f32[2,256,256]{2,1,0:T(8,128)S(1)} collective-permute-done((f32[2,256,256]{2,1,0:T(8,128)S(1)}, f32[2,256,256]{2,1,0:T(8,128)S(1)}, u32[]{:S(2)}, u32[]{:S(2)}) %collective-permute-start.11) | collective-permute-done | bytes 524320 | tf_op jit(solution)/shard_map/ppermute | solution.py:29
  1560.3 2.4 broadcast_select_fusion.1
  (161 shorter events, 85.0 us)
Async XLA Ops:
  7.2 501.0 %all-reduce.30.cloned.1.call-start = ((), (), s32[]{:S(2)}) async-start(), calls=%async_computation.2 | async-start | bytes 278528 | tf_op jit(solution)/shard_map/psum | solution.py:160
  118.7 392.0 %collective-permute-start = (f32[4096]{0:T(1024)S(1)}, f32[4096]{0:T(1024)S(1)}, u32[]{:S(2)}, u32[]{:S(2)}) collective-permute-start(f32[4096]{0:T(1024)S(1)} %multiply_add_fusion.10), channel_id=1, source_target_pairs={{0,16},{1,17},{2,18},{3,19},{4,20},{5,21},{6,22},{7,23},{8,24},{9,... | collective-permute-start | bytes 49160 | tf_op jit(solution)/shard_map/ppermute | solution.py:29
  478.4 901.7 %all-reduce.26.cloned.1.call-start = ((), (), s32[]{:S(2)}) async-start(), calls=%async_computation | async-start | bytes 191488 | tf_op jit(solution)/shard_map/psum | solution.py:194
  524.0 864.8 %copy-start.70 = (f32[4,256]{1,0:T(4,128)S(1)}, f32[4,256]{1,0:T(4,128)}, u32[]{:S(2)}) copy-start(f32[4,256]{1,0:T(4,128)} %param.57) | copy-start | bytes 12292
  524.0 864.8 %copy-start.81 = (f32[4,256]{1,0:T(4,128)S(1)}, f32[4,256]{1,0:T(4,128)}, u32[]{:S(2)}) copy-start(f32[4,256]{1,0:T(4,128)} %param.62) | copy-start | bytes 12292
  524.0 866.1 %copy-start.27 = (f32[1,2,24,256]{3,2,1,0:T(8,128)S(1)}, f32[1,2,24,256]{3,2,1,0:T(8,128)}, u32[]{:S(2)}) copy-start(f32[1,2,24,256]{3,2,1,0:T(8,128)} %param.46) | copy-start | bytes 147460
  524.0 866.1 %copy-start.68 = (f32[2,24,256]{2,1,0:T(8,128)S(1)}, f32[2,24,256]{2,1,0:T(8,128)}, u32[]{:S(2)}) copy-start(f32[2,24,256]{2,1,0:T(8,128)} %param.49) | copy-start | bytes 147460
  524.1 866.1 %copy-start.69 = (f32[2,24,256]{2,1,0:T(8,128)S(1)}, f32[2,24,256]{2,1,0:T(8,128)}, u32[]{:S(2)}) copy-start(f32[2,24,256]{2,1,0:T(8,128)} %param.50) | copy-start | bytes 147460
  526.4 930.0 %copy-start.15 = (f32[1,2,2,256,256]{4,3,2,1,0:T(8,128)S(1)}, f32[1,2,2,256,256]{4,3,2,1,0:T(8,128)}, u32[]{:S(2)}) copy-start(f32[1,2,2,256,256]{4,3,2,1,0:T(8,128)} %param.47) | copy-start | bytes 3145732
  526.4 930.0 %copy-start.42 = (f32[2,2,256,256]{3,2,1,0:T(8,128)S(1)}, f32[2,2,256,256]{3,2,1,0:T(8,128)}, u32[]{:S(2)}) copy-start(f32[2,2,256,256]{3,2,1,0:T(8,128)} %param.51) | copy-start | bytes 3145732
  526.4 930.0 %copy-start.43 = (f32[2,2,256,256]{3,2,1,0:T(8,128)S(1)}, f32[2,2,256,256]{3,2,1,0:T(8,128)}, u32[]{:S(2)}) copy-start(f32[2,2,256,256]{3,2,1,0:T(8,128)} %param.52) | copy-start | bytes 3145732
  535.8 917.3 %all-reduce.28.cloned.1.call-start = ((), (), s32[]{:S(2)}) async-start(), calls=%async_computation.1 | async-start | bytes 3145728 | tf_op jit(solution)/shard_map/psum | solution.py:194
  1381.0 50.5 %collective-permute-start.14 = (f32[29,256]{1,0:T(8,128)S(1)}, f32[29,256]{1,0:T(8,128)}, u32[]{:S(2)}, u32[]{:S(2)}) collective-permute-start(f32[29,256]{1,0:T(8,128)S(1)} %get-tuple-element.2569), channel_id=1, source_target_pairs={{16,0},{17,1},{18,2},{19,3},{20,4},{21,5},{22,6},{23,7},{24,8},{25... | collective-permute-start | bytes 89096 | tf_op jit(solution)/shard_map/ppermute | solution.py:29
  1382.3 51.9 %collective-permute-start.13 = (f32[29,256]{1,0:T(8,128)S(1)}, f32[29,256]{1,0:T(8,128)}, u32[]{:S(2)}, u32[]{:S(2)}) collective-permute-start(f32[29,256]{1,0:T(8,128)S(1)} %get-tuple-element.2568), channel_id=1, source_target_pairs={{16,0},{17,1},{18,2},{19,3},{20,4},{21,5},{22,6},{23,7},{24,8},{25... | collective-permute-start | bytes 89096 | tf_op jit(solution)/shard_map/ppermute | solution.py:29
  1383.6 73.7 %collective-permute-start.10 = (f32[29,256]{1,0:T(8,128)S(1)}, f32[29,256]{1,0:T(8,128)}, u32[]{:S(2)}, u32[]{:S(2)}) collective-permute-start(f32[29,256]{1,0:T(8,128)S(1)} %get-tuple-element.2567), channel_id=1, source_target_pairs={{16,0},{17,1},{18,2},{19,3},{20,4},{21,5},{22,6},{23,7},{24,8},{25... | collective-permute-start | bytes 89096 | tf_op jit(solution)/shard_map/ppermute | solution.py:29
  1386.2 40.5 %collective-permute-start.8 = (f32[2,4,256]{2,1,0:T(4,128)}, f32[2,4,256]{2,1,0:T(4,128)}, u32[]{:S(2)}, u32[]{:S(2)}) collective-permute-start(f32[2,4,256]{2,1,0:T(4,128)} %get-tuple-element.2572), channel_id=1, source_target_pairs={{16,0},{17,1},{18,2},{19,3},{20,4},{21,5},{22,6},{23,7},{24,8},{25... | collective-permute-start | bytes 24584 | tf_op jit(solution)/shard_map/ppermute | solution.py:29
  1387.5 8.0 collective-permute-start.20
  1395.5 5.7 collective-permute-start.19
  1401.2 5.7 collective-permute-start.18
  1406.9 5.7 collective-permute-start.17
  1412.6 5.7 collective-permute-start.12
  1418.3 5.7 collective-permute-start.3
  1424.0 5.5 collective-permute-start.9
  1426.7 31.9 %collective-permute-start.1 = (f32[2,24,256]{2,1,0:T(8,128)S(1)}, f32[2,24,256]{2,1,0:T(8,128)S(1)}, u32[]{:S(2)}, u32[]{:S(2)}) collective-permute-start(f32[2,24,256]{2,1,0:T(8,128)S(1)} %get-tuple-element.2577), channel_id=1, source_target_pairs={{16,0},{17,1},{18,2},{19,3},{20,4},{21,5},{22,6},{23,7},{24,8},{25... | collective-permute-start | bytes 147464 | tf_op jit(solution)/shard_map/ppermute | solution.py:29
  1429.5 30.3 %collective-permute-start.4 = (f32[2,24,256]{2,1,0:T(8,128)S(1)}, f32[2,24,256]{2,1,0:T(8,128)S(1)}, u32[]{:S(2)}, u32[]{:S(2)}) collective-permute-start(f32[2,24,256]{2,1,0:T(8,128)S(1)} %get-tuple-element.2578), channel_id=1, source_target_pairs={{16,0},{17,1},{18,2},{19,3},{20,4},{21,5},{22,6},{23,7},{24,8},{25... | collective-permute-start | bytes 147464 | tf_op jit(solution)/shard_map/ppermute | solution.py:29
  1431.4 29.7 %collective-permute-start.5 = (f32[2,24,256]{2,1,0:T(8,128)S(1)}, f32[2,24,256]{2,1,0:T(8,128)}, u32[]{:S(2)}, u32[]{:S(2)}) collective-permute-start(f32[2,24,256]{2,1,0:T(8,128)S(1)} %get-tuple-element.2579), channel_id=1, source_target_pairs={{16,0},{17,1},{18,2},{19,3},{20,4},{21,5},{22,6},{23,7},{24,8},{25... | collective-permute-start | bytes 147464 | tf_op jit(solution)/shard_map/ppermute | solution.py:29
  1455.1 16.8 %collective-permute-start.16 = (f32[2,256,256]{2,1,0:T(8,128)S(1)}, f32[2,256,256]{2,1,0:T(8,128)S(1)}, u32[]{:S(2)}, u32[]{:S(2)}) collective-permute-start(f32[2,256,256]{2,1,0:T(8,128)S(1)} %get-tuple-element.2566), channel_id=1, source_target_pairs={{16,0},{17,1},{18,2},{19,3},{20,4},{21,5},{22,6},{23,7},{24,8},{25... | collective-permute-start | bytes 1572872 | tf_op jit(solution)/shard_map/ppermute | solution.py:29
  1457.3 25.8 %collective-permute-start.15 = (f32[2,256,256]{2,1,0:T(8,128)S(1)}, f32[2,256,256]{2,1,0:T(8,128)S(1)}, u32[]{:S(2)}, u32[]{:S(2)}) collective-permute-start(f32[2,256,256]{2,1,0:T(8,128)S(1)} %get-tuple-element.2565), channel_id=1, source_target_pairs={{16,0},{17,1},{18,2},{19,3},{20,4},{21,5},{22,6},{23,7},{24,8},{25... | collective-permute-start | bytes 1572872 | tf_op jit(solution)/shard_map/ppermute | solution.py:29
  1458.6 101.7 %collective-permute-start.2 = (f32[2,2,256,256]{3,2,1,0:T(8,128)S(1)}, f32[2,2,256,256]{3,2,1,0:T(8,128)S(1)}, u32[]{:S(2)}, u32[]{:S(2)}) collective-permute-start(f32[2,2,256,256]{3,2,1,0:T(8,128)S(1)} %get-tuple-element.2574), channel_id=1, source_target_pairs={{16,0},{17,1},{18,2},{19,3},{20,4},{21,5},{22,6},{23,7},{24,8},{25... | collective-permute-start | bytes 3145736 | tf_op jit(solution)/shard_map/ppermute | solution.py:29
  1459.9 100.4 %collective-permute-start.6 = (f32[2,2,256,256]{3,2,1,0:T(8,128)S(1)}, f32[2,2,256,256]{3,2,1,0:T(8,128)S(1)}, u32[]{:S(2)}, u32[]{:S(2)}) collective-permute-start(f32[2,2,256,256]{3,2,1,0:T(8,128)S(1)} %get-tuple-element.2575), channel_id=1, source_target_pairs={{16,0},{17,1},{18,2},{19,3},{20,4},{21,5},{22,6},{23,7},{24,8},{25... | collective-permute-start | bytes 3145736 | tf_op jit(solution)/shard_map/ppermute | solution.py:29
  1461.2 99.1 %collective-permute-start.7 = (f32[2,2,256,256]{3,2,1,0:T(8,128)S(1)}, f32[2,2,256,256]{3,2,1,0:T(8,128)S(1)}, u32[]{:S(2)}, u32[]{:S(2)}) collective-permute-start(f32[2,2,256,256]{3,2,1,0:T(8,128)S(1)} %get-tuple-element.2576), channel_id=1, source_target_pairs={{16,0},{17,1},{18,2},{19,3},{20,4},{21,5},{22,6},{23,7},{24,8},{25... | collective-permute-start | bytes 3145736 | tf_op jit(solution)/shard_map/ppermute | solution.py:29
  1471.9 87.5 %collective-permute-start.11 = (f32[2,256,256]{2,1,0:T(8,128)S(1)}, f32[2,256,256]{2,1,0:T(8,128)S(1)}, u32[]{:S(2)}, u32[]{:S(2)}) collective-permute-start(f32[2,256,256]{2,1,0:T(8,128)S(1)} %get-tuple-element.2564), channel_id=1, source_target_pairs={{16,0},{17,1},{18,2},{19,3},{20,4},{21,5},{22,6},{23,7},{24,8},{25... | collective-permute-start | bytes 1572872 | tf_op jit(solution)/shard_map/ppermute | solution.py:29
  (17 other events, 6276.7 us)
Sparse Core Ops, SparseCore 0:
  478.6 29.5 all-reduce.29
  535.9 844.1 all-reduce.25
  1383.7 69.3 all-reduce.27
where the time goes:
time: 1580 us; the launch traced here: 1570 us
  waiting for transfers between devices  990 us (63%)
  starting transfers between devices  381 us (24%)
  matrix products  58.4 us (4%)
  other arithmetic  48.9 us (3%)
  loops' own time  35.9 us (2%)
  blocking collectives  25.7 us (2%)
    psum x2, waiting for transfers between devices, body(): lax.psum((pieces[0], pieces[1], pieces[2], pieces[3], pieces[4], pieces[5...  860 us
    ppermute x21, starting transfers between devices, from_behind(): return lax.ppermute(shard, axis, pairs)  381 us
    ppermute x21, waiting for transfers between devices, from_behind(): return lax.ppermute(shard, axis, pairs)  115 us
    dot_general x12, matrix products, matmul(): return jnp.dot(left, right, precision=lax.Precision.HIGHEST)  58.4 us
  transfers between devices with their start and end apart: 24, of which 13 were waited for; matrix products, arithmetic and copies ran while one was open for 2% of the time, Pallas kernels for 0%

commit v1 on v0

v1 whole, which is shorter than its diff:
```python
import functools

import jax
import jax.numpy as jnp
from jax import lax
from jax.experimental import pallas as pl
from jax.experimental.pallas import tpu as pltpu
from jax.sharding import PartitionSpec as P

OBS = 17
ACT = 6
HID = 256
STEP = 5
BLOCK = 1024

GAMMA = 0.99
ALPHA = 0.2
ETA = 1.0
LEARN = 0.03
BETA_ONE = 0.5
BETA_TWO = 0.5
DECAY = 0.01
EPS = 1e-08
TAU = 0.05
HALF_LOG_TWO_PI = 0.9189385332046727
LOG_TWO = 0.6931471805599453

F32 = jnp.float32
BF16 = jnp.bfloat16

ROW_OBS, ROW_NEXT, ROW_ACT, ROW_NOISE, ROW_NOISE2, ROW_SCAL, ROWS = 0, 24, 48, 56, 64, 72, 80


def dot(a, b):
    return lax.dot_general(a, b, (((1,), (0,)), ((), ())), preferred_element_type=F32)


def dot_t(a, b):
    return lax.dot_general(a, b, (((1,), (1,)), ((), ())), preferred_element_type=F32)


def split(w):
    high = w.astype(BF16).astype(F32)
    return high, w - high


def halves(p):
    n = p.shape[0] // 2
    return p[:n] + p[n:]


def prep_input(stage, w1, edge, bias, n_in):
    stage[...] = jnp.zeros_like(stage)
    stage[0:OBS, :] = edge[0:OBS, :]
    stage[OBS : OBS + 1, :] = bias[0:1, :]
    if n_in > OBS:
        stage[24 : 24 + ACT, :] = edge[OBS : OBS + ACT, :]
    high, low = split(0.5 * stage[0:32, :])
    w1[...] = jnp.concatenate([high, low], 0).T.astype(BF16)


def prep_hidden(fwd, bwd, hidden):
    w = 0.5 * hidden
    if fwd is not None:
        high, low = split(w.T)
        fwd[...] = jnp.concatenate([high, low], 0).astype(BF16)
    if bwd is not None:
        high, low = split(w)
        bwd[...] = jnp.concatenate([high, low], 0).astype(BF16)


def silu_half(u):
    t = jnp.tanh(u)
    return u + u * t, t


def kernel(
    n_dp,
    rows,
    x_in, c_edge, c_hidden, c_bias, a_edge, a_hidden, a_bias,
    out_c, out_a,
    x_b, pi_b, pi_act, stage, vec, tvec, avec,
    p_edge, p_hidden, p_bias,
    w1, f0, f1, b0, b1, ga, t1w, eq,
    tw1, tf0, tf1, teq,
    aw1, af0, af1, ab0, ab1, ao, aot,
    h1x, h2x, h3s, s1, s2, s3, k1, k2, k3, d1s, d2s, d3s,
    ah1x, ah2x, ah3, as1, as2, as3, heads,
    value, unit_f, unit_out, unit_in, dg_b, dv_b,
    slope_out, slope_in, q_own, least, least_in, target,
    acc_h1, acc_h1t, acc_h0, acc_h0t, acc_x, acc_t, acc_last, acc_o,
    sem_param_s, sem_param_r, sem_pi_s, sem_pi_r, sem_least_s, sem_least_r, sem_unit_s, sem_unit_r, sem_slope_s, sem_slope_r,
):
    g = lax.axis_index("grp")
    e = lax.axis_index("ens")
    me = g * 4 + e
    blocks = rows // BLOCK
    half = rows // 2
    online = g == 1
    targetd = g == 0

    def dev(gg, ee):
        return {"grp": gg, "ens": ee}

    def remote(src, dst, send, recv, where):
        return pltpu.make_async_remote_copy(
            src_ref=src, dst_ref=dst, send_sem=send, recv_sem=recv, device_id=where, device_id_type=pl.DeviceIdType.MESH
        )

    barrier = pltpu.get_barrier_semaphore()
    for k in range(1, 8):
        p = lax.rem(me + k, 8)
        pl.semaphore_signal(barrier, inc=1, device_id=dev(p // 4, lax.rem(p, 4)), device_id_type=pl.DeviceIdType.MESH)
    pl.semaphore_wait(barrier, 7)

    def param_copies():
        where = dev(0, e)
        return [
            remote(c_edge.at[1], p_edge, sem_param_s.at[0], sem_param_r.at[0], where),
            remote(c_bias.at[1], p_bias, sem_param_s.at[1], sem_param_r.at[1], where),
            remote(c_hidden.at[1, 0], p_hidden.at[0], sem_param_s.at[2], sem_param_r.at[2], where),
            remote(c_hidden.at[1, 1], p_hidden.at[1], sem_param_s.at[3], sem_param_r.at[3], where),
        ]

    @pl.when(online)
    def _():
        for c in param_copies():
            c.start()

    obs = x_in[ROW_OBS : ROW_OBS + 24, :]
    xin = jnp.concatenate([obs, x_in[ROW_ACT : ROW_ACT + 8, :]], 0).astype(BF16)
    x_b[0:32, :] = xin
    x_b[32:64, :] = xin

    def prep_critic(edge, hid0, hid1, bias, w1_, f0_, f1_, b0_, b1_, vec_, eq_, ga_, t1_):
        prep_input(stage, w1_, edge, bias, OBS + ACT)
        prep_hidden(f0_, b0_, hid0[...])
        prep_hidden(f1_, b1_, hid1[...])
        stage[...] = jnp.zeros_like(stage)
        stage[0:1, :] = 0.5 * bias[1:2, :]
        stage[1:2, :] = 0.5 * bias[2:3, :]
        stage[2:3, :] = edge[23:24, :]
        vec_[...] = stage[...].T
        stage[...] = jnp.zeros_like(stage)
        high, low = split(edge[23:24, :])
        stage[0:1, :] = high
        stage[1:2, :] = low
        eq_[...] = stage[0:16, :].astype(BF16)
        if ga_ is not None:
            stage[...] = jnp.zeros_like(stage)
            stage[0:ACT, :] = 0.5 * edge[OBS : OBS + ACT, :]
            high, low = split(stage[0:8, :])
            both = jnp.concatenate([high, low], 0)
            ga_[...] = both.astype(BF16)
            stage[0:16, :] = both
            t1_[...] = stage[...].T[:, 0:16].astype(BF16)

    def prep_actor():
        prep_input(stage, aw1, a_edge, a_bias, OBS)
        prep_hidden(af0, ab0, a_hidden[0])
        prep_hidden(af1, ab1, a_hidden[1])
        stage[...] = jnp.zeros_like(stage)
        stage[0:1, :] = 0.5 * a_bias[1:2, :]
        stage[1:2, :] = 0.5 * a_bias[2:3, :]
        stage[2:3, :] = a_bias[3:4, :]
        avec[...] = stage[...].T
        stage[...] = jnp.zeros_like(stage)
        stage[0:ACT, :] = a_edge[OBS : OBS + ACT, :]
        stage[8 : 8 + ACT, :] = a_edge[OBS + ACT : OBS + 2 * ACT, :]
        high, low = split(stage[0:16, :])
        both = jnp.concatenate([high, low], 0)
        ao[...] = both.astype(BF16)
        stage[0:32, :] = both
        aot[...] = stage[...].T[:, 0:32].astype(BF16)

    prep_actor()

    def actor_block(src, sl, noise_row, keep):
        u = dot(aw1[...], src[:, sl])
        h, t = silu_half(u)
        hb = h.astype(BF16)
        if keep:
            ah1x[0:HID, sl] = hb
            as1[:, sl] = ((1.0 + t) + h * (1.0 - t)).astype(BF16)
        u = halves(dot(af0[...], hb)) + avec[:, 0:1]
        h, t = silu_half(u)
        hb = h.astype(BF16)
        if keep:
            ah2x[0:HID, sl] = hb
            as2[:, sl] = ((1.0 + t) + h * (1.0 - t)).astype(BF16)
        u = halves(dot(af1[...], hb)) + avec[:, 1:2]
        h, t = silu_half(u)
        hb = h.astype(BF16)
        if keep:
            ah3[:, sl] = hb
            as3[:, sl] = ((1.0 + t) + h * (1.0 - t)).astype(BF16)
        out = halves(dot(ao[...], hb))
        eps = x_in[noise_row : noise_row + 8, sl]
        ok = (lax.broadcasted_iota(jnp.int32, (8, 1), 0) < ACT).astype(F32)
        center = out[0:8] + avec[0:8, 2:3] * ok
        th = jnp.tanh(out[8:16] + avec[6:14, 2:3] * ok)
        log_std = 3.5 * th - 1.5
        spread_e = jnp.exp(log_std) * eps
        latent = center + spread_e
        soft = jnp.maximum(-2.0 * latent, 0.0) + jnp.log(1.0 + jnp.exp(-2.0 * jnp.abs(latent)))
        terms = -0.5 * eps * eps - log_std - HALF_LOG_TWO_PI - 2.0 * (LOG_TWO - latent - soft)
        logp = jnp.sum(terms * ok, axis=0, keepdims=True)
        sample = jnp.tanh(latent) * ok
        return sample, logp, th, spread_e

    @pl.when(online)
    def _():
        ones = (lax.broadcasted_iota(jnp.int32, (16, rows), 0) == 0).astype(BF16)
        ah1x[HID : HID + 16, :] = ones
        ah2x[HID : HID + 16, :] = ones

        def body(i, _):
            sl = pl.ds(pl.multiple_of(i * BLOCK, BLOCK), BLOCK)
            sample, logp, th, spread_e = actor_block(x_b, sl, ROW_NOISE, True)
            pi_act[:, sl] = sample
            heads[0:8, sl] = th
            heads[8:16, sl] = spread_e
            heads[16:17, sl] = logp
            return 0

        lax.fori_loop(0, blocks, body, 0)
        remote(pi_act, pi_act, sem_pi_s, sem_pi_r, dev(0, e)).start()
        prep_critic(c_edge.at[0], c_hidden.at[0, 0], c_hidden.at[0, 1], c_bias.at[0], w1, f0, f1, b0, b1, vec, eq, ga, t1w)
        vec[0:1, 8:9] = c_bias[0, 3:4, 0:1]

    def least_copies():
        out = []
        for k in range(1, 4):
            out.append(remote(least, least_in.at[k], sem_least_s.at[k], sem_least_r.at[k], dev(0, lax.rem(e + k, 4))))
        for k in range(4):
            out.append(remote(least, least_in.at[k], sem_least_s.at[4 + k], sem_least_r.at[k], dev(1, lax.rem(e + k, 4))))
        return out

    @pl.when(targetd)
    def _():
        for m in range(2):
            prep_critic(
                c_edge.at[m], c_hidden.at[m, 0], c_hidden.at[m, 1], c_bias.at[m],
                tw1.at[m], tf0.at[m], tf1.at[m], None, None, tvec.at[m], teq.at[m], None, None,
            )
            tvec[m, 0:1, 8:9] = c_bias[m, 3:4, 0:1]
        pi_b[0:32, :] = jnp.concatenate([x_in[ROW_NEXT : ROW_NEXT + 24, :], jnp.zeros((8, rows), F32)], 0).astype(BF16)
        pi_b[32:64, :] = pi_b[0:32, :]

        def body(i, _):
            sl = pl.ds(pl.multiple_of(i * BLOCK, BLOCK), BLOCK)
            sample, logp, th, spread_e = actor_block(pi_b, sl, ROW_NOISE2, False)
            nx = jnp.concatenate([x_in[ROW_NEXT : ROW_NEXT + 24, sl], sample], 0).astype(BF16)
            nx = jnp.concatenate([nx, nx], 0)
            low = None
            for m in range(2):
                h, t = silu_half(dot(tw1[m], nx))
                h, t = silu_half(halves(dot(tf0[m], h.astype(BF16))) + tvec[m, :, 0:1])
                h, t = silu_half(halves(dot(tf1[m], h.astype(BF16))) + tvec[m, :, 1:2])
                r = dot(teq[m], h.astype(BF16))
                q = r[0:1] + r[1:2] + tvec[m, 0:1, 8:9]
                low = q if low is None else jnp.minimum(low, q)
            least[:, sl] = low - ALPHA * logp
            return 0

        lax.fori_loop(0, blocks, body, 0)
        for c in least_copies():
            c.start()
        for c in param_copies():
            c.wait_recv()
        prep_critic(p_edge, p_hidden.at[0], p_hidden.at[1], p_bias, w1, f0, f1, b0, b1, vec, eq, ga, t1w)
        vec[0:1, 8:9] = p_bias[3:4, 0:1]

    ones = (lax.broadcasted_iota(jnp.int32, (16, rows), 0) == 0).astype(BF16)
    h1x[HID : HID + 16, :] = ones
    h2x[HID : HID + 16, :] = ones

    def curves(u):
        h, t = silu_half(u)
        c = 1.0 + t
        d = 1.0 - t
        return h, c + h * d, (c * d) * (1.0 - u * t)

    def body_a(i, _):
        sl = pl.ds(pl.multiple_of(i * BLOCK, BLOCK), BLOCK)
        h, a1, q1 = curves(dot(w1[...], x_b[:, sl]))
        hb = h.astype(BF16)
        h1x[0:HID, sl] = hb
        s1[:, sl] = a1.astype(BF16)
        h, a2, q2 = curves(halves(dot(f0[...], hb)) + vec[:, 0:1])
        hb = h.astype(BF16)
        h2x[0:HID, sl] = hb
        s2[:, sl] = a2.astype(BF16)
        h, a3, q3 = curves(halves(dot(f1[...], hb)) + vec[:, 1:2])
        hb = h.astype(BF16)
        h3s[:, sl] = hb
        s3[:, sl] = a3.astype(BF16)
        r = dot(eq[...], hb)
        value[:, sl] = r[0:1] + r[1:2] + vec[0:1, 8:9]
        last = vec[:, 2:3]
        db = (last * a3).astype(BF16)
        d3s[:, sl] = db
        k3[:, sl] = (last * q3).astype(BF16)
        m = halves(dot(b1[...], db))
        db = (m * a2).astype(BF16)
        d2s[:, sl] = db
        k2[:, sl] = (m * q2).astype(BF16)
        m = halves(dot(b0[...], db))
        db = (m * a1).astype(BF16)
        d1s[:, sl] = db
        k1[:, sl] = (m * q1).astype(BF16)
        slope = halves(dot(ga[...], db))
        inv = lax.rsqrt(jnp.sum(slope * slope, axis=0, keepdims=True) + 0.01)
        unit_f[0:8, sl] = slope * inv
        unit_f[8:9, sl] = inv
        return 0

    lax.fori_loop(0, blocks, body_a, 0)
    unit_out[...] = jnp.concatenate([unit_f[0:8, 0:half], unit_f[0:8, half:rows]], 0).astype(BF16)

    def unit_copies():
        out = []
        for k in range(1, 8):
            p = lax.rem(me + k, 8)
            out.append(
                remote(unit_out, unit_in.at[k - 1], sem_unit_s.at[k - 1], sem_unit_r.at[k - 1], dev(p // 4, lax.rem(p, 4)))
            )
        return out

    for c in unit_copies():
        c.start()

    @pl.when(targetd)
    def _():
        remote(pi_act, pi_act, sem_pi_s, sem_pi_r, dev(0, e)).wait_recv()

    pin = jnp.concatenate([obs, pi_act[...]], 0).astype(BF16)
    pi_b[0:32, :] = pin
    pi_b[32:64, :] = pin

    def body_p(i, _):
        sl = pl.ds(pl.multiple_of(i * BLOCK, BLOCK), BLOCK)

        def act(u):
            h, t = silu_half(u)
            hb, tb = h.astype(BF16), t.astype(BF16)
            one = jnp.ones((), BF16)
            return hb, (one + tb) + hb * (one - tb)

        h, a1 = act(dot(w1[...], pi_b[:, sl]))
        h, a2 = act(dot(f0[0:HID, :], h) + vec[:, 0:1])
        h, a3 = act(dot(f1[0:HID, :], h) + vec[:, 1:2])
        r = dot(eq[...], h)
        q_own[:, sl] = r[0:1] + r[1:2] + vec[0:1, 8:9]
        d = vec[:, 2:3].astype(BF16) * a3
        d = dot(b1[0:HID, :], d).astype(BF16) * a2
        d = dot(b0[0:HID, :], d).astype(BF16) * a1
        slope = halves(dot(ga[...], d))
        unit_f[16:24, sl] = slope
        return 0

    lax.fori_loop(0, blocks, body_p, 0)
    rid = lax.broadcasted_iota(jnp.int32, (8, 1), 0)
    packed = unit_f[16:24, :] + jnp.where(rid == 6, q_own[...], 0.0)
    slope_out[...] = jnp.concatenate([packed[:, 0:half], packed[:, half:rows]], 0).astype(BF16)

    def slope_copy(k):
        return remote(slope_out, slope_in.at[me_slot(k)], sem_slope_s.at[k], sem_slope_r.at[me_slot(k)], dev(1, lax.rem(e + k, 4)))

    def me_slot(k):
        return g * 4 + k

    @pl.when(targetd)
    def _():
        slope_copy(0).start()

    for k in range(1, 4):
        slope_copy(k).start()

    @pl.when(targetd)
    def _():
        least_in[0] = least[...]
        for c in least_copies()[:3]:
            c.wait_recv()

    @pl.when(online)
    def _():
        for c in least_copies()[3:]:
            c.wait_recv()

    low = jnp.minimum(jnp.minimum(least_in[0], least_in[1]), jnp.minimum(least_in[2], least_in[3]))
    scal = x_in[ROW_SCAL : ROW_SCAL + 8, :]
    target[...] = scal[0:1] + scal[1:2] * low

    for c in unit_copies():
        c.wait_recv()
    spread = unit_out[...].astype(F32)
    for k in range(7):
        spread = spread + unit_in[k].astype(F32)
    spread = jnp.concatenate([spread[0:8], spread[8:16]], 1)
    unit = unit_f[0:8, :]
    inv = unit_f[8:9, :]
    valid = scal[2:3]
    critics = 8
    d_unit = (2.0 * ETA / (critics - 1)) * valid * (spread - unit)
    along = jnp.sum(d_unit * unit, axis=0, keepdims=True)
    dg = (d_unit - unit * along) * inv
    gap = value[...] - target[...]
    dv = 2.0 * valid * gap
    diverse = jnp.sum(valid * jnp.sum(unit * (spread - unit), axis=0, keepdims=True), axis=1, keepdims=True)
    errors = jnp.sum(valid * gap * gap, axis=1, keepdims=True)
    dv_sum = jnp.sum(dv, axis=1, keepdims=True)
    dgb = dg.astype(BF16)
    dg_b[...] = jnp.concatenate([dgb, dgb], 0)
    rid16 = lax.broadcasted_iota(jnp.int32, (16, 1), 0)
    dv_b[...] = jnp.where(rid16 == 0, dv, jnp.where(rid16 == 1, 1.0, 0.0)).astype(BF16)

    for acc in (acc_h1, acc_h1t, acc_h0, acc_h0t, acc_x, acc_t, acc_last):
        acc[...] = jnp.zeros_like(acc)

    def body_b(i, _):
        sl = pl.ds(pl.multiple_of(i * BLOCK, BLOCK), BLOCK)
        a1, a2, a3 = s1[:, sl], s2[:, sl], s3[:, sl]
        rows_dv = dv_b[:, sl]
        dvh = (rows_dv[0:1].astype(F32) * 0.5).astype(BF16)
        tp1 = dot(t1w[...], dg_b[:, sl]).astype(BF16)
        th1 = a1 * tp1
        tp2 = halves(dot(f0[...], th1)).astype(BF16)
        th2 = a2 * tp2
        tp3 = halves(dot(f1[...], th2)).astype(BF16)
        th3 = a3 * tp3
        d3 = d3s[:, sl]
        ap3 = dvh * d3 + k3[:, sl] * tp3
        last = dot_t(rows_dv, h3s[:, sl])
        lone = dot_t(rows_dv, th3)
        acc_last[...] += last[0:8] + jnp.where(rid == 0, lone[1:2], 0.0)
        acc_h1[...] += dot_t(h2x[:, sl], ap3)
        acc_h1t[...] += dot_t(th2, d3)
        ah = halves(dot(b1[...], ap3)).astype(BF16)
        ap2 = a2 * ah + k2[:, sl] * tp2
        acc_h0[...] += dot_t(h1x[:, sl], ap2)
        acc_h0t[...] += dot_t(th1, d2s[:, sl])
        ah = halves(dot(b0[...], ap2)).astype(BF16)
        ap1 = a1 * ah + k1[:, sl] * tp1
        acc_x[...] += dot_t(x_b[0:32, sl], ap1)
        acc_t[...] += dot_t(dg_b[:, sl], d1s[:, sl])
        return 0

    lax.fori_loop(0, blocks, body_b, 0)
    out_c[0:HID, :] = acc_h0[0:HID, :] + 0.5 * acc_h0t[...]
    out_c[HID : 2 * HID, :] = acc_h1[0:HID, :] + 0.5 * acc_h1t[...]
    rid32 = lax.broadcasted_iota(jnp.int32, (32, 1), 0)
    lane = lax.broadcasted_iota(jnp.int32, (1, HID), 1)
    stats = jnp.where(lane == 0, dv_sum, jnp.where(lane == 1, errors, jnp.where(lane == 2, diverse, 0.0)))
    small = acc_x[...]
    small = small + jnp.where(rid32 == 18, acc_h0[HID : HID + 1, :], 0.0)
    small = small + jnp.where(rid32 == 19, acc_h1[HID : HID + 1, :], 0.0)
    small = small + jnp.where(rid32 == 20, stats, 0.0)
    small = small + jnp.where(rid32 == 23, acc_last[0:1, :], 0.0)
    out_c[2 * HID : 2 * HID + 24, :] = small[0:24]
    out_c[2 * HID + 24 : 2 * HID + 32, :] = small[24:32] + 0.5 * acc_t[0:8, :]

    @pl.when(targetd)
    def _():
        out_a[...] = jnp.zeros_like(out_a)

    @pl.when(online)
    def _():
        total = slope_out[...].astype(F32)
        for k in range(4):
            remote(slope_out, slope_in.at[k], sem_slope_s.at[0], sem_slope_r.at[k], dev(1, e)).wait_recv()
            total = total + slope_in[k].astype(F32)
        for k in range(5, 8):
            remote(slope_out, slope_in.at[k], sem_slope_s.at[0], sem_slope_r.at[k], dev(1, e)).wait_recv()
            total = total + slope_in[k].astype(F32)
        total = jnp.concatenate([total[0:8], total[8:16]], 1) * (1.0 / critics)
        valid = x_in[ROW_SCAL + 2 : ROW_SCAL + 3, :]
        d_sample = -valid * total
        d_logp = ALPHA * valid
        sample = pi_act[...]
        th = heads[0:8, :]
        spread_e = heads[8:16, :]
        eps = x_in[ROW_NOISE : ROW_NOISE + 8, :]
        ok = (rid < ACT).astype(F32)
        dz = (d_sample * (1.0 - sample * sample) + d_logp * 2.0 * sample) * ok
        dls = (dz * spread_e - d_logp) * (3.5 * (1.0 - th * th)) * ok
        dout = jnp.concatenate([dz, dls], 0).astype(BF16)
        heads[24:40, :] = dout.astype(F32)
        logp = heads[16:17, :]
        actor_sum = jnp.sum(valid * (ALPHA * logp - total[6:7]), axis=1, keepdims=True)
        count = jnp.sum(valid, axis=1, keepdims=True)
        for acc in (acc_h1, acc_h0, acc_x, acc_o):
            acc[...] = jnp.zeros_like(acc)

        def body_c(i, _):
            sl = pl.ds(pl.multiple_of(i * BLOCK, BLOCK), BLOCK)
            do = heads[24:40, sl].astype(BF16)
            h3 = ah3[:, sl]
            acc_o[0:16, :] += dot_t(do, h3)
            d3 = (dot(aot[...], jnp.concatenate([do, do], 0)) * (0.5 * as3[:, sl].astype(F32))).astype(BF16)
            acc_h1[...] += dot_t(ah2x[:, sl], d3)
            d2 = (halves(dot(ab1[...], d3)) * as2[:, sl].astype(F32)).astype(BF16)
            acc_h0[...] += dot_t(ah1x[:, sl], d2)
            d1 = (halves(dot(ab0[...], d2)) * as1[:, sl].astype(F32)).astype(BF16)
            acc_x[...] += dot_t(x_b[0:32, sl], d1)
            one = (lax.broadcasted_iota(jnp.int32, (16, BLOCK), 0) == 0).astype(BF16)
            acc_o[16:32, 0:128] += dot_t(one, jnp.concatenate([do, jnp.zeros((112, BLOCK), BF16)], 0))
            return 0

        lax.fori_loop(0, blocks, body_c, 0)
        out_a[0:HID, :] = acc_h0[0:HID, :]
        out_a[HID : 2 * HID, :] = acc_h1[0:HID, :]
        stats = jnp.where(lane == 0, actor_sum, jnp.where(lane == 1, count, 0.0))
        small = acc_x[...]
        small = small + jnp.where(rid32 == 18, acc_h0[HID : HID + 1, :], 0.0)
        small = small + jnp.where(rid32 == 19, acc_h1[HID : HID + 1, :], 0.0)
        small = small + jnp.where(rid32 == 20, acc_o[16:17, :], 0.0)
        small = small + jnp.where(rid32 == 21, stats, 0.0)
        out_a[2 * HID : 2 * HID + 32, :] = small
        out_a[2 * HID + 32 : 2 * HID + 48, :] = acc_o[0:16, :]

    @pl.when(online)
    def _():
        for c in param_copies():
            c.wait_send()
        remote(pi_act, pi_act, sem_pi_s, sem_pi_r, dev(0, e)).wait_send()

    @pl.when(targetd)
    def _():
        for c in least_copies():
            c.wait_send()
        slope_copy(0).wait_send()

    for k in range(1, 4):
        slope_copy(k).wait_send()
    for c in unit_copies():
        c.wait_send()


def fused(n_dp, rows, packed, own, aparams):
    v = pltpu.VMEM
    big = lambda n=HID: v((n, rows), BF16)
    dma = pltpu.SemaphoreType.DMA
    scratch = [
        v((64, rows), BF16), v((64, rows), BF16), v((8, rows), F32),
        v((128, HID), F32), v((HID, 128), F32), v((2, HID, 128), F32), v((HID, 128), F32),
        v((24, HID), F32), v((2, HID, HID), F32), v((4, HID), F32),
        v((HID, 64), BF16), v((512, HID), BF16), v((512, HID), BF16), v((512, HID), BF16), v((512, HID), BF16),
        v((16, HID), BF16), v((HID, 16), BF16), v((16, HID), BF16),
        v((2, HID, 64), BF16), v((2, 512, HID), BF16), v((2, 512, HID), BF16), v((2, 16, HID), BF16),
        v((HID, 64), BF16), v((512, HID), BF16), v((512, HID), BF16), v((512, HID), BF16), v((512, HID), BF16),
        v((32, HID), BF16), v((HID, 32), BF16),
        big(272), big(272), big(), big(), big(), big(), big(), big(), big(), big(), big(), big(),
        big(272), big(272), big(), v((HID, rows), BF16), v((HID, rows), BF16), v((HID, rows), BF16), v((40, rows), F32),
        v((1, rows), F32), v((24, rows), F32), v((16, rows // 2), BF16), v((7, 16, rows // 2), BF16),
        v((16, rows), BF16), v((16, rows), BF16),
        v((16, rows // 2), BF16), v((8, 16, rows // 2), BF16), v((1, rows), F32),
        v((1, rows), F32), v((4, 1, rows), F32), v((1, rows), F32),
        v((272, HID), F32), v((HID, HID), F32), v((272, HID), F32), v((HID, HID), F32),
        v((32, HID), F32), v((16, HID), F32), v((8, HID), F32), v((32, HID), F32),
        dma((4,)), dma((4,)), dma, dma, dma((8,)), dma((4,)), dma((7,)), dma((7,)), dma((4,)), dma((8,)),
    ]
    spec = pl.BlockSpec(memory_space=pltpu.VMEM)
    return pl.pallas_call(
        functools.partial(kernel, n_dp, rows),
        out_shape=(jax.ShapeDtypeStruct((544, HID), F32), jax.ShapeDtypeStruct((560, HID), F32)),
        in_specs=[spec] * 7,
        out_specs=(spec, spec),
        scratch_shapes=scratch,
        compiler_params=pltpu.CompilerParams(collective_id=0, has_side_effects=True, vmem_limit_bytes=62 * 2**20),
        name="edac_gradients",
    )(packed, *own, *aparams)


def adamw(param, grad, first, second):
    first_new = BETA_ONE * first + (1.0 - BETA_ONE) * grad
    second_new = BETA_TWO * second + (1.0 - BETA_TWO) * grad * grad
    ratio = first_new / (1.0 - BETA_ONE**STEP) / (jnp.sqrt(second_new / (1.0 - BETA_TWO**STEP)) + EPS)
    return (param - LEARN * (ratio + DECAY * param), first_new, second_new)


def body(
    n_dp,
    states, actions, rewards, done, noise, counts,
    crit_edge, crit_hidden, crit_bias, edge_m, edge_v, hidden_m, hidden_v, bias_m, bias_v,
    act_edge, act_hidden, act_bias, act_edge_m, act_edge_v, act_hidden_m, act_hidden_v, act_bias_m, act_bias_v,
):
    rows = states.shape[0]
    online = lax.axis_index("grp") == 1
    own = (crit_edge[0], crit_hidden[0], crit_bias[0])
    aparams = (act_edge, act_hidden, act_bias)
    valid = (jnp.arange(rows, dtype=jnp.int32) < counts[0]).astype(F32)
    states_t, actions_t, noise_t = states.T, actions.T, noise.T
    zero = lambda n: jnp.zeros((n, rows), F32)
    one = jnp.ones((1, rows), F32)
    packed = jnp.concatenate(
        [
            states_t[:OBS], one, zero(6), states_t[OBS:], one, zero(6),
            actions_t, zero(2), noise_t[:ACT], zero(2), noise_t[ACT:], zero(2),
            rewards[None], GAMMA * (1.0 - done.astype(F32))[None], valid[None], zero(5),
        ],
        0,
    )
    grad_c, grad_a = fused(n_dp, rows, packed, own, aparams)
    grad_c, grad_a = lax.psum((grad_c, grad_a), "dp")
    both = lax.all_gather(grad_c, "grp")[::-1]
    grad_a = lax.psum(grad_a, "grp")
    total = grad_a[2 * HID + 21, 1]
    scale = 1.0 / total
    small = both[:, 2 * HID :]
    g_edge = jnp.concatenate([small[:, 0:OBS], small[:, 24 : 24 + ACT], small[:, 23:24]], 1) * scale
    g_hidden = both[:, : 2 * HID].reshape(2, 2, HID, HID) * scale
    lane = jnp.arange(HID) == 0
    g_bias = jnp.concatenate([small[:, 17:20], jnp.where(lane, small[:, 20:21], 0.0)], 1) * scale
    member_sums = small[:, 20, 1:3]
    smalla = grad_a[2 * HID :]
    ga_edge = jnp.concatenate([smalla[0:OBS], smalla[32 : 32 + ACT], smalla[40 : 40 + ACT]], 0) * scale
    ga_hidden = grad_a[: 2 * HID].reshape(2, HID, HID) * scale
    out_bias = jnp.concatenate([smalla[20, 0:ACT], smalla[20, 8 : 8 + ACT], jnp.zeros((HID - 2 * ACT,), F32)])[None]
    ga_bias = jnp.concatenate([smalla[17:20], out_bias], 0) * scale
    actor_sums = smalla[21, 0:2]
    onl = [lax.ppermute(p, "grp", [(1, 0)]) for p in own]
    onl = [jnp.where(online, a, b) for a, b in zip(own, onl)]
    outs, moments = [], []
    for p, mine, grad, m, v in zip(onl, own, (g_edge, g_hidden, g_bias), (edge_m, hidden_m, bias_m), (edge_v, hidden_v, bias_v)):
        master, m_new, v_new = adamw(p, grad, m, v)
        polyak = TAU * master.astype(BF16).astype(F32) + (1.0 - TAU) * mine
        outs.append(jnp.where(online, master, polyak)[None])
        moments += [m_new, v_new]
    aouts, amoments = [], []
    for p, grad, m, v in zip(
        aparams, (ga_edge, ga_hidden, ga_bias), (act_edge_m, act_hidden_m, act_bias_m), (act_edge_v, act_hidden_v, act_bias_v)
    ):
        master, m_new, v_new = adamw(p, grad, m, v)
        aouts.append(master)
        amoments += [m_new, v_new]
    return (*outs, *moments, *aouts, *amoments, member_sums, actor_sums)


def solution(mesh):
    member = P("grp", "ens", None, None)
    hidden = P("grp", "ens", None, None, None)
    mom = P("ens", None, None)
    mom_h = P("ens", None, None, None)
    return jax.shard_map(
        functools.partial(body, mesh.shape["dp"]),
        mesh=mesh,
        in_specs=(
            P("dp", None), P("dp", None), P("dp"), P("dp"), P("dp", None), P("dp"),
            member, hidden, member, mom, mom, mom_h, mom_h, mom, mom,
        ) + (P(),) * 9,
        out_specs=(member, hidden, member, mom, mom, mom_h, mom_h, mom, mom) + (P(),) * 9 + (P("ens", None), P()),
        check_vma=False,
    )
```

time: 1580 us -> 211 us (0.13)
  waiting for transfers between devices: 990 us -> 113 us
  starting transfers between devices: 381 us -> 4.13 us
  matrix products: 58.4 us -> 0 us
  Pallas kernels: 0 us -> 48.2 us
  other arithmetic: 48.9 us -> 10 us
  loops' own time: 35.9 us -> 0 us
  blocking collectives: 25.7 us -> 0 us
    psum x3 -> x2, waiting for transfers between devices: 875 us -> 101 us  [the longest x1 62.3 us: body(): grad_c, grad_a = lax.psum((grad_c, grad_a), 'dp')]
    ppermute x21 -> x3, starting transfers between devices: 381 us -> 4.01 us  [body(): onl = [lax.ppermute(p, 'grp', [(1, 0)]) for p in own]]
    ppermute x21 -> x3, waiting for transfers between devices: 115 us -> 0.01 us  [body(): onl = [lax.ppermute(p, 'grp', [(1, 0)]) for p in own]]
    dot_general x12 -> x0, matrix products: 58.4 us -> none  [matmul(): return jnp.dot(left, right, precision=lax.Precision.HIGHEST)]
    pallas_call x0 -> x1, Pallas kernels: none -> 48.2 us  [fused(): pl.pallas_call(functools.partial(kernel, n_dp, rows), out_shape=(jax.Shap...]
    another operation x3 -> x0, loops' own time: 35.9 us -> none  [the longest x1 31.5 us: body(): lax.cond(online, online_side, target_side)]
  transfers between devices with their start and end apart: 24 -> 6, of which waited for: 13 -> 3; matrix products, arithmetic and copies ran while one was open for 2% -> 7% of each run, Pallas kernels for 0% -> 0%
where the time goes in v1:
time: 211 us; the launch traced here: 210 us
  waiting for transfers between devices  113 us (54%)
  Pallas kernels  48.2 us (23%)
  local copies, waits for them, and re-layouts  19.6 us (9%)
  between operations  15.5 us (7%)
  other arithmetic  10 us (5%)
  starting transfers between devices  4.13 us (2%)
    psum x1, waiting for transfers between devices, body(): grad_c, grad_a = lax.psum((grad_c, grad_a), 'dp')  62.3 us
    pallas_call x1, Pallas kernels, fused(): pl.pallas_call(functools.partial(kernel, n_dp, rows), out_shape=(jax.Shap...  48.2 us
    psum x1, waiting for transfers between devices, body(): grad_a = lax.psum(grad_a, 'grp')  38.3 us
    all_gather x1, waiting for transfers between devices, body(): both = lax.all_gather(grad_c, 'grp')[::-1]  12.2 us
    concatenate x1, local copies, waits for them, and re-layouts, body(): jnp.concatenate([states_t[:OBS], one, zero(6), states_t[OBS:], one, zero(...  8.73 us
    broadcast_in_dim x3, other arithmetic, body(): outs.append(jnp.where(online, master, polyak)[None])  5.3 us
  transfers between devices with their start and end apart: 6, of which 3 were waited for; matrix products, arithmetic and copies ran while one was open for 7% of the time, Pallas kernels for 0%

profile of v1, /device:TPU:0, one launch (start us, length us, event | category | flops | bytes accessed | tf_op | source)
XLA Modules:
  0.0 210.3 jit_solution(6645019909394060865)
XLA Ops:
  7.2 0.0 all-reduce.6.cloned.1.call-start
  7.9 0.7 subtract_multiply_fusion
  8.6 1.0 fusion.15
  9.7 1.2 fusion.13
  11.0 8.7 %concatenate.18.x_in = f32[80,4096]{1,0:T(8,128)} concatenate(f32[17,4096]{1,0:T(8,128)S(1)} %get-tuple-element.47, f32[1,4096]{1,0:T(1,128)S(1)} %broadcast_in_dim.34, f32[6,4096]{1,0:T(8,128)S(1)} %broadcast.67, f32[17,4096]{1,0:T(8,128)S(1)} %get-tuple-element.46, f32[1,4096]{1,0:T(1,128)S(1)} %broadcast_in_dim.34, f32[6,4096]{1,0:T(8,128)S(1)} %broadcast.67, ...), dimensions={0} | concatenate | bytes 2621440 | tf_op jit(solution)/shard_map/concatenate | solution.py:596
  19.7 48.2 %edac_gradients.1 = (f32[544,256]{1,0:T(8,128)}, f32[560,256]{1,0:T(8,128)}) custom-call(f32[80,4096]{1,0:T(8,128)} %concatenate.18.x_in, f32[2,24,256]{2,1,0:T(8,128)} %bitcast.38, f32[2,2,256,256]{3,2,1,0:T(8,128)} %bitcast.32, f32[2,4,256]{2,1,0:T(4,128)} %bitcast.42, f32[29,256]{1,0:T(8,128)} %a_edge.1, f32[2,256,256]{2,1,0:T(8,128)} %a_hidden.1, ...), custom_call_target="tpu_custom_call" | custom-call | tf_op jit(solution)/shard_map/edac_gradients/pallas_call | solution.py:564
  68.0 0.0 all-reduce.4.cloned.1.call-start
  68.1 62.3 %all-reduce.6.cloned.1.call-done = (f32[560,256]{1,0:T(8,128)}, f32[1,544,256]{2,1,0:T(8,128)}) async-done(((f32[560,256]{1,0:T(8,128)}, f32[1,544,256]{2,1,0:T(8,128)}), (f32[560,256]{1,0:T(8,128)}, f32[1,544,256]{2,1,0:T(8,128)})) %all-reduce.6.cloned.1.call-update) | async-done | bytes 1130512 | tf_op jit(solution)/shard_map/psum | solution.py:605
  130.5 1.4 collective-permute-start.2
  131.9 1.3 collective-permute-start
  133.2 1.3 collective-permute-start.1
  134.6 38.3 %all-reduce.4.cloned.1.call-done = f32[560,256]{1,0:T(8,128)} async-done(((f32[560,256]{1,0:T(8,128)}), f32[560,256]{1,0:T(8,128)}) %all-reduce.4.cloned.1.call-update) | async-done | bytes 573456 | tf_op jit(solution)/shard_map/psum | solution.py:607
  172.9 1.3 slice.131
  174.9 0.8 slice_bitcast_fusion.2
  175.7 0.1 pad_maximum_fusion
  175.8 0.7 slice.139
  176.5 0.6 multiply_subtract_fusion.5
  177.1 0.7 fusion.14
  177.8 0.7 slice.135
  178.6 0.7 multiply_subtract_fusion.3
  179.2 1.2 slice_bitcast_fusion
  180.4 1.1 slice_multiply_fusion
  181.6 1.4 multiply_subtract_fusion.1
  183.0 12.2 %all-gather.2.cloned.1.call-done = f32[2,544,256]{2,1,0:T(8,128)} async-done(((f32[1,544,256]{2,1,0:T(8,128)}), f32[2,544,256]{2,1,0:T(8,128)}) %all-gather.2.cloned.1.call-update) | async-done | bytes 1114128 | tf_op jit(solution)/shard_map/all_gather | solution.py:606
  195.2 1.2 slice-done
  196.4 0.1 reverse_multiply_fusion
  196.5 1.2 copy-done.1
  197.8 4.0 %select_bitcast_fusion = (f32[1,2,2,256,256]{4,3,2,1,0:T(8,128)}, f32[2,2,256,256]{3,2,1,0:T(8,128)}, f32[2,2,256,256]{3,2,1,0:T(8,128)}) fusion(f32[2,2,256,256]{3,2,1,0:T(8,128)} %collective-permute-done.1, pred[]{:T(512)S(6)} %eq.9, f32[1,2,2,256,256]{4,3,2,1,0:T(8,128)S(1)} %copy-done, f32[2,2,256,256]{3,2,1,0:T(8,128)S(1)} %bitcast.31, ...), kind=kLoop, calls=%fused_computation.3 | loop fusion | flops 5505024 | bytes 8388609 | tf_op jit(solution)/shard_map/broadcast_in_dim | solution.py:628
  201.8 0.6 select_bitcast_fusion.2
  202.4 0.1 slice.142
  202.5 0.6 slice.122
  203.1 0.7 select_bitcast_fusion.1
  (65 shorter events, 0.3 us)
Async XLA Ops:
  7.2 123.2 %all-reduce.6.cloned.1.call-start = ((), (), s32[]{:S(2)}) async-start(), calls=%async_computation.2 | async-start | bytes 2260992 | tf_op jit(solution)/shard_map/psum | solution.py:605
  8.6 2.3 %copy-start.8 = (f32[4096,6]{0,1:T(8,128)S(1)}, f32[4096,6]{0,1:T(8,128)}, u32[]{:S(2)}) copy-start(f32[4096,6]{0,1:T(8,128)} %param.25) | copy-start | bytes 294916
  8.6 2.3 %copy-start.14 = (f32[4096]{0:T(1024)S(1)}, f32[4096]{0:T(1024)}, u32[]{:S(2)}) copy-start(f32[4096]{0:T(1024)} %param.26) | copy-start | bytes 49156
  67.9 62.6 %copy-start.11 = (f32[1,2,4,256]{3,2,1,0:T(4,128)S(1)}, f32[1,2,4,256]{3,2,1,0:T(4,128)}, u32[]{:S(2)}) copy-start(f32[1,2,4,256]{3,2,1,0:T(4,128)} %param.32) | copy-start | bytes 24580
  67.9 64.0 %copy-start.6 = (f32[1,2,24,256]{3,2,1,0:T(8,128)S(1)}, f32[1,2,24,256]{3,2,1,0:T(8,128)}, u32[]{:S(2)}) copy-start(f32[1,2,24,256]{3,2,1,0:T(8,128)} %param.30) | copy-start | bytes 147460
  67.9 65.3 %copy-start = (f32[1,2,2,256,256]{4,3,2,1,0:T(8,128)S(1)}, f32[1,2,2,256,256]{4,3,2,1,0:T(8,128)}, u32[]{:S(2)}) copy-start(f32[1,2,2,256,256]{4,3,2,1,0:T(8,128)} %param.31) | copy-start | bytes 3145732
  67.9 108.6 %copy-start.15 = (f32[4,256]{1,0:T(4,128)S(1)}, f32[4,256]{1,0:T(4,128)}, u32[]{:S(2)}) copy-start(f32[4,256]{1,0:T(4,128)} %a_bias.1) | copy-start | bytes 12292
  67.9 108.5 %copy-start.18 = (f32[4,256]{1,0:T(4,128)S(1)}, f32[4,256]{1,0:T(4,128)}, u32[]{:S(2)}) copy-start(f32[4,256]{1,0:T(4,128)} %param.46) | copy-start | bytes 12292
  68.0 108.5 %copy-start.19 = (f32[4,256]{1,0:T(4,128)S(1)}, f32[4,256]{1,0:T(4,128)}, u32[]{:S(2)}) copy-start(f32[4,256]{1,0:T(4,128)} %param.47) | copy-start | bytes 12292
  68.0 110.6 %copy-start.7 = (f32[29,256]{1,0:T(8,128)S(1)}, f32[29,256]{1,0:T(8,128)}, u32[]{:S(2)}) copy-start(f32[29,256]{1,0:T(8,128)} %a_edge.1) | copy-start | bytes 89092
  68.0 110.6 %copy-start.12 = (f32[29,256]{1,0:T(8,128)S(1)}, f32[29,256]{1,0:T(8,128)}, u32[]{:S(2)}) copy-start(f32[29,256]{1,0:T(8,128)} %param.42) | copy-start | bytes 89092
  68.0 110.6 %copy-start.13 = (f32[29,256]{1,0:T(8,128)S(1)}, f32[29,256]{1,0:T(8,128)}, u32[]{:S(2)}) copy-start(f32[29,256]{1,0:T(8,128)} %param.43) | copy-start | bytes 89092
  68.0 104.9 %all-reduce.4.cloned.1.call-start = ((), (), s32[]{:S(2)}) async-start(), calls=%async_computation.1 | async-start | bytes 1146880 | tf_op jit(solution)/shard_map/psum | solution.py:607
  130.4 51.2 %copy-start.2 = (f32[2,256,256]{2,1,0:T(8,128)S(1)}, f32[2,256,256]{2,1,0:T(8,128)}, u32[]{:S(2)}) copy-start(f32[2,256,256]{2,1,0:T(8,128)} %a_hidden.1) | copy-start | bytes 1572868
  130.4 51.2 %copy-start.4 = (f32[2,256,256]{2,1,0:T(8,128)S(1)}, f32[2,256,256]{2,1,0:T(8,128)}, u32[]{:S(2)}) copy-start(f32[2,256,256]{2,1,0:T(8,128)} %param.44) | copy-start | bytes 1572868
  130.4 51.2 %copy-start.5 = (f32[2,256,256]{2,1,0:T(8,128)S(1)}, f32[2,256,256]{2,1,0:T(8,128)}, u32[]{:S(2)}) copy-start(f32[2,256,256]{2,1,0:T(8,128)} %param.45) | copy-start | bytes 1572868
  130.4 64.8 %all-gather.2.cloned.1.call-start = ((), (), s32[]{:S(2)}) async-start(), calls=%async_computation | async-start | bytes 1671168 | tf_op jit(solution)/shard_map/all_gather | solution.py:606
  130.5 71.3 %collective-permute-start.2 = (f32[2,4,256]{2,1,0:T(4,128)S(1)}, f32[2,4,256]{2,1,0:T(4,128)S(1)}, u32[]{:S(2)}, u32[]{:S(2)}) collective-permute-start(f32[2,4,256]{2,1,0:T(4,128)S(1)} %bitcast.43), channel_id=1, source_target_pairs={{16,0},{17,1},{18,2},{19,3},{20,4},{21,5},{22,6},{23,7},{24,8},{25... | collective-permute-start | bytes 24584 | tf_op jit(solution)/shard_map/ppermute | solution.py:622
  131.9 71.2 %collective-permute-start = (f32[2,24,256]{2,1,0:T(8,128)S(1)}, f32[2,24,256]{2,1,0:T(8,128)S(1)}, u32[]{:S(2)}, u32[]{:S(2)}) collective-permute-start(f32[2,24,256]{2,1,0:T(8,128)S(1)} %bitcast.39), channel_id=1, source_target_pairs={{16,0},{17,1},{18,2},{19,3},{20,4},{21,5},{22,6},{23,7},{24,8},{25... | collective-permute-start | bytes 147464 | tf_op jit(solution)/shard_map/ppermute | solution.py:622
  133.2 64.4 %collective-permute-start.1 = (f32[2,2,256,256]{3,2,1,0:T(8,128)S(1)}, f32[2,2,256,256]{3,2,1,0:T(8,128)}, u32[]{:S(2)}, u32[]{:S(2)}) collective-permute-start(f32[2,2,256,256]{3,2,1,0:T(8,128)S(1)} %bitcast.33), channel_id=1, source_target_pairs={{16,0},{17,1},{18,2},{19,3},{20,4},{21,5},{22,6},{23,7},{24,8},{25... | collective-permute-start | bytes 3145736 | tf_op jit(solution)/shard_map/ppermute | solution.py:622
  195.2 1.2 slice-start
  195.2 2.5 %copy-start.3 = (f32[2,2,256,256]{3,2,1,0:T(8,128)S(1)}, f32[2,2,256,256]{3,2,1,0:T(8,128)}, u32[]{:S(2)}) copy-start(f32[2,2,256,256]{3,2,1,0:T(8,128)} %param.35) | copy-start | bytes 3145732
  196.4 1.2 copy-start.1
  197.7 4.1 %copy-start.16 = (f32[2,4,256]{2,1,0:T(4,128)S(1)}, f32[2,4,256]{2,1,0:T(4,128)}, u32[]{:S(2)}) copy-start(f32[2,4,256]{2,1,0:T(4,128)} %param.37) | copy-start | bytes 24580
  197.7 4.1 %copy-start.17 = (f32[2,4,256]{2,1,0:T(4,128)S(1)}, f32[2,4,256]{2,1,0:T(4,128)}, u32[]{:S(2)}) copy-start(f32[2,4,256]{2,1,0:T(4,128)} %param.38) | copy-start | bytes 24580
  197.7 5.4 %slice-start.1 = ((f32[2,544,256]{2,1,0:T(8,128)}), f32[2,6,256]{2,1,0:T(8,128)S(1)}, s32[]{:S(2)}) async-start(f32[2,544,256]{2,1,0:T(8,128)} %all-gather.2.cloned.1.call-done), calls=%async_computation.4 | async-start | bytes 32768 | tf_op jit(solution)/shard_map/slice | solution.py:611
  197.7 5.3 %slice-start.2 = ((f32[2,544,256]{2,1,0:T(8,128)}), f32[2,17,256]{2,1,0:T(8,128)S(1)}, s32[]{:S(2)}) async-start(f32[2,544,256]{2,1,0:T(8,128)} %all-gather.2.cloned.1.call-done), calls=%async_computation.5 | async-start | bytes 98304 | tf_op jit(solution)/shard_map/slice | solution.py:611
  197.7 5.4 %copy-start.9 = (f32[2,24,256]{2,1,0:T(8,128)S(1)}, f32[2,24,256]{2,1,0:T(8,128)}, u32[]{:S(2)}) copy-start(f32[2,24,256]{2,1,0:T(8,128)} %param.33) | copy-start | bytes 147460
  197.7 5.4 %copy-start.10 = (f32[2,24,256]{2,1,0:T(8,128)S(1)}, f32[2,24,256]{2,1,0:T(8,128)}, u32[]{:S(2)}) copy-start(f32[2,24,256]{2,1,0:T(8,128)} %param.34) | copy-start | bytes 147460
Sparse Core Ops, SparseCore 0:
  68.1 62.1 all-reduce.5
  132.7 40.1 all-reduce.3
  174.5 20.6 all-gather.1

commit v2 on v1

v2 whole, which is shorter than its diff:
```python
import functools

import jax
import jax.numpy as jnp
from jax import lax
from jax.experimental import pallas as pl
from jax.experimental.pallas import tpu as pltpu
from jax.sharding import PartitionSpec as P

OBS = 17
ACT = 6
HID = 256
STEP = 5
BLOCK = 1024

GAMMA = 0.99
ALPHA = 0.2
ETA = 1.0
LEARN = 0.03
BETA_ONE = 0.5
BETA_TWO = 0.5
DECAY = 0.01
EPS = 1e-08
TAU = 0.05
HALF_LOG_TWO_PI = 0.9189385332046727
LOG_TWO = 0.6931471805599453

F32 = jnp.float32
BF16 = jnp.bfloat16

CRITIC_SMALL, ACTOR_SMALL = 32, 64


def dot(a, b):
    return lax.dot_general(a, b, (((1,), (0,)), ((), ())), preferred_element_type=F32)


def dot_t(a, b):
    return lax.dot_general(a, b, (((1,), (1,)), ((), ())), preferred_element_type=F32)


def split(w):
    high = w.astype(BF16).astype(F32)
    return high, w - high


def halves(p):
    n = p.shape[0] // 2
    return p[:n] + p[n:]


def prep_input(stage, w1, edge, bias, n_in):
    stage[...] = jnp.zeros_like(stage)
    stage[0:OBS, :] = edge[0:OBS, :]
    stage[OBS : OBS + 1, :] = bias[0:1, :]
    if n_in > OBS:
        stage[24 : 24 + ACT, :] = edge[OBS : OBS + ACT, :]
    high, low = split(0.5 * stage[0:32, :])
    w1[...] = jnp.concatenate([high, low], 0).T.astype(BF16)


def prep_hidden(fwd, bwd, hidden):
    w = 0.5 * hidden
    if fwd is not None:
        high, low = split(w.T)
        fwd[...] = jnp.concatenate([high, low], 0).astype(BF16)
    if bwd is not None:
        high, low = split(w)
        bwd[...] = jnp.concatenate([high, low], 0).astype(BF16)


def silu_half(u):
    t = jnp.tanh(u)
    return u + u * t, t


def up(n, by):
    return -(-n // by) * by


def kernel(
    n_dp,
    rows,
    keep,
    states, actions, noise, rewards, done, counts, c_edge, c_hidden, c_bias, a_edge, a_hidden, a_bias,
    out_c, out_a, out_pe, out_ph, out_pb,
    xs, ns, eps_s, x_b, pi_b, pi_act, stage, vec, tvec, avec,
    p_edge, p_hidden, p_bias,
    w1, f0, f1, b0, b1, ga, t1w, eq,
    tw1, tf0, tf1, teq,
    aw1, af0, af1, ab0, ab1, ao, aot,
    h1x, h2x, h3s, s1, s2, s3, k1, k2, k3, d1s, d2s, d3s,
    heads,
    value, unit_f, unit_out, unit_in, dg_b, dv_b,
    slope_out, slope_in, q_own, least, least_in, target,
    acc_h1, acc_h1t, acc_h0, acc_h0t, acc_x, acc_t, acc_last, acc_o,
    part_c, part_a, sum_c, sum_a, in_h1, in_h0, in_sm, in_ac,
    sem_param_s, sem_param_r, sem_pi_s, sem_pi_r, sem_least_s, sem_least_r, sem_unit_s, sem_unit_r, sem_slope_s, sem_slope_r,
    rs_s, rs_r, ag_s, ag_r, xf_s, xf_r, ef_s, ef_r, sem_out,
):
    g = lax.axis_index("grp")
    e = lax.axis_index("ens")
    z = lax.axis_index("dp")
    me = g * 4 + e
    blocks = rows // BLOCK
    half = rows // 2
    online = g == 1
    targetd = g == 0
    critics = 8

    def dev(gg, ee):
        return {"grp": gg, "ens": ee}

    def remote(src, dst, send, recv, where):
        return pltpu.make_async_remote_copy(
            src_ref=src, dst_ref=dst, send_sem=send, recv_sem=recv, device_id=where, device_id_type=pl.DeviceIdType.MESH
        )

    barrier = pltpu.get_barrier_semaphore()
    for k in range(1, 8):
        p = lax.rem(me + k, 8)
        pl.semaphore_signal(barrier, inc=1, device_id=dev(p // 4, lax.rem(p, 4)), device_id_type=pl.DeviceIdType.MESH)
    for k in range(1, n_dp):
        pl.semaphore_signal(barrier, inc=1, device_id={"dp": lax.rem(z + k, n_dp)}, device_id_type=pl.DeviceIdType.MESH)
    pl.semaphore_wait(barrier, 7 + n_dp - 1)

    def param_copy(m, what):
        where = dev(0, e)
        src, dst = (
            (c_edge.at[m], p_edge.at[m]),
            (c_bias.at[m], p_bias.at[m]),
            (c_hidden.at[m, 0], p_hidden.at[m, 0]),
            (c_hidden.at[m, 1], p_hidden.at[m, 1]),
        )[what]
        return remote(src, dst, sem_param_s.at[m, what], sem_param_r.at[m, what], where)

    @pl.when(online)
    def _():
        for m in (1, 0):
            for what in range(4):
                param_copy(m, what).start()

    ones_row = jnp.ones((1, rows), F32)
    xs[...] = jnp.zeros_like(xs)
    xs[0:OBS, :] = states[0:OBS, :]
    xs[OBS : OBS + 1, :] = ones_row
    xs[24 : 24 + ACT, :] = actions[...]
    eps_s[...] = jnp.zeros_like(eps_s)
    xin = xs[...].astype(BF16)
    x_b[0:32, :] = xin
    x_b[32:64, :] = xin

    @pl.when(online)
    def _():
        eps_s[0:ACT, :] = noise[0:ACT, :]

    @pl.when(targetd)
    def _():
        eps_s[0:ACT, :] = noise[ACT : 2 * ACT, :]
        ns[...] = jnp.zeros_like(ns)
        ns[0:OBS, :] = states[OBS : 2 * OBS, :]
        ns[OBS : OBS + 1, :] = ones_row

    row_id = lax.broadcasted_iota(jnp.int32, (1, rows), 1)
    valid = jnp.where(row_id < counts[0], 1.0, 0.0)

    def prep_critic(edge, hid0, hid1, bias, w1_, f0_, f1_, b0_, b1_, vec_, eq_, ga_, t1_):
        prep_input(stage, w1_, edge, bias, OBS + ACT)
        prep_hidden(f0_, b0_, hid0[...])
        prep_hidden(f1_, b1_, hid1[...])
        stage[...] = jnp.zeros_like(stage)
        stage[0:1, :] = 0.5 * bias[1:2, :]
        stage[1:2, :] = 0.5 * bias[2:3, :]
        stage[2:3, :] = edge[23:24, :]
        vec_[...] = stage[...].T
        vec_[0:1, 8:9] = bias[3:4, 0:1]
        stage[...] = jnp.zeros_like(stage)
        high, low = split(edge[23:24, :])
        stage[0:1, :] = high
        stage[1:2, :] = low
        eq_[...] = stage[0:16, :].astype(BF16)
        if ga_ is not None:
            stage[...] = jnp.zeros_like(stage)
            stage[0:ACT, :] = 0.5 * edge[OBS : OBS + ACT, :]
            high, low = split(stage[0:8, :])
            both = jnp.concatenate([high, low], 0)
            ga_[...] = both.astype(BF16)
            stage[0:16, :] = both
            t1_[...] = stage[...].T[:, 0:16].astype(BF16)

    def prep_actor():
        prep_input(stage, aw1, a_edge, a_bias, OBS)
        prep_hidden(af0, ab0, a_hidden[0])
        prep_hidden(af1, ab1, a_hidden[1])
        stage[...] = jnp.zeros_like(stage)
        stage[0:1, :] = 0.5 * a_bias[1:2, :]
        stage[1:2, :] = 0.5 * a_bias[2:3, :]
        stage[2:3, :] = a_bias[3:4, :]
        avec[...] = stage[...].T
        stage[...] = jnp.zeros_like(stage)
        stage[0:ACT, :] = a_edge[OBS : OBS + ACT, :]
        stage[8 : 8 + ACT, :] = a_edge[OBS + ACT : OBS + 2 * ACT, :]
        high, low = split(stage[0:16, :])
        ao[...] = jnp.concatenate([high, low], 0).astype(BF16)
        stage[...] = jnp.zeros_like(stage)
        stage[0 : 2 * ACT, :] = a_edge[OBS : OBS + 2 * ACT, :]
        high, low = split(stage[0:16, :])
        stage[0:32, :] = jnp.concatenate([high, low], 0)
        aot[...] = stage[...].T[:, 0:32].astype(BF16)

    prep_actor()

    def actor_layers(src):
        kept = []
        hb = None
        for w, b in ((aw1, None), (af0, 0), (af1, 1)):
            u = dot(w[...], src) if b is None else halves(dot(w[...], hb)) + avec[:, b : b + 1]
            h, t = silu_half(u)
            hb = h.astype(BF16)
            kept.append((hb, h, t))
        return kept

    ok8 = (lax.broadcasted_iota(jnp.int32, (8, 1), 0) < ACT).astype(F32)

    def actor_heads(hb, sl):
        out = halves(dot(ao[...], hb))
        eps = eps_s[:, sl]
        center = out[0:8] + avec[0:8, 2:3] * ok8
        th = jnp.tanh(out[8:16] + avec[6:14, 2:3] * ok8)
        log_std = 3.5 * th - 1.5
        spread_e = jnp.exp(log_std) * eps
        latent = center + spread_e
        soft = jnp.maximum(-2.0 * latent, 0.0) + jnp.log(1.0 + jnp.exp(-2.0 * jnp.abs(latent)))
        terms = -0.5 * eps * eps - log_std - HALF_LOG_TWO_PI - 2.0 * (LOG_TWO - latent - soft)
        logp = jnp.sum(terms * ok8, axis=0, keepdims=True)
        sample = jnp.tanh(latent) * ok8
        return sample, logp, th, spread_e

    @pl.when(online)
    def _():
        def body(i, _):
            sl = pl.ds(pl.multiple_of(i * BLOCK, BLOCK), BLOCK)
            kept = actor_layers(x_b[:, sl])
            sample, logp, th, spread_e = actor_heads(kept[2][0], sl)
            pi_act[:, sl] = sample
            heads[0:8, sl] = th
            heads[8:16, sl] = spread_e
            heads[16:17, sl] = logp
            return 0

        lax.fori_loop(0, blocks, body, 0)
        remote(pi_act, pi_act, sem_pi_s, sem_pi_r, dev(0, e)).start()
        prep_critic(c_edge.at[0], c_hidden.at[0, 0], c_hidden.at[0, 1], c_bias.at[0], w1, f0, f1, b0, b1, vec, eq, ga, t1w)

    def least_online(k):
        return remote(least, least_in.at[k], sem_least_s.at[4 + k], sem_least_r.at[k], dev(1, lax.rem(e + k, 4)))

    def least_target(k):
        return remote(least, least_in.at[k], sem_least_s.at[k], sem_least_r.at[k], dev(0, lax.rem(e + k, 4)))

    @pl.when(targetd)
    def _():
        for m in range(2):
            prep_critic(
                c_edge.at[m], c_hidden.at[m, 0], c_hidden.at[m, 1], c_bias.at[m],
                tw1.at[m], tf0.at[m], tf1.at[m], None, None, tvec.at[m], teq.at[m], None, None,
            )

        def body(i, _):
            sl = pl.ds(pl.multiple_of(i * BLOCK, BLOCK), BLOCK)
            nx = ns[:, sl].astype(BF16)
            kept = actor_layers(jnp.concatenate([nx, nx], 0))
            sample, logp, th, spread_e = actor_heads(kept[2][0], sl)
            nx = jnp.concatenate([ns[0:24, sl], sample], 0).astype(BF16)
            nx = jnp.concatenate([nx, nx], 0)
            low = None
            for m in range(2):
                h, t = silu_half(dot(tw1[m], nx))
                h, t = silu_half(halves(dot(tf0[m], h.astype(BF16))) + tvec[m, :, 0:1])
                h, t = silu_half(halves(dot(tf1[m], h.astype(BF16))) + tvec[m, :, 1:2])
                r = dot(teq[m], h.astype(BF16))
                q = r[0:1] + r[1:2] + tvec[m, 0:1, 8:9]
                low = q if low is None else jnp.minimum(low, q)
            least[:, sl] = low - ALPHA * logp
            return 0

        lax.fori_loop(0, blocks, body, 0)
        for k in range(1, 4):
            least_target(k).start()
        for k in range(4):
            least_online(k).start()
        for what in range(4):
            param_copy(1, what).wait_recv()
        prep_critic(p_edge.at[1], p_hidden.at[1, 0], p_hidden.at[1, 1], p_bias.at[1], w1, f0, f1, b0, b1, vec, eq, ga, t1w)
        remote(pi_act, pi_act, sem_pi_s, sem_pi_r, dev(0, e)).wait_recv()

    pin = jnp.concatenate([xs[0:24, :], pi_act[...]], 0).astype(BF16)
    pi_b[0:32, :] = pin
    pi_b[32:64, :] = pin

    def body_p(i, _):
        sl = pl.ds(pl.multiple_of(i * BLOCK, BLOCK), BLOCK)

        def act(u):
            h, t = silu_half(u)
            hb, tb = h.astype(BF16), t.astype(BF16)
            one = jnp.ones((), BF16)
            return hb, (one + tb) + hb * (one - tb)

        h, a1 = act(dot(w1[...], pi_b[:, sl]))
        h, a2 = act(dot(f0[0:HID, :], h) + vec[:, 0:1])
        h, a3 = act(dot(f1[0:HID, :], h) + vec[:, 1:2])
        r = dot(eq[...], h)
        q_own[:, sl] = r[0:1] + r[1:2] + vec[0:1, 8:9]
        d = vec[:, 2:3].astype(BF16) * a3
        d = dot(b1[0:HID, :], d).astype(BF16) * a2
        d = dot(b0[0:HID, :], d).astype(BF16) * a1
        unit_f[16:24, sl] = halves(dot(ga[...], d))
        return 0

    lax.fori_loop(0, blocks, body_p, 0)
    rid = lax.broadcasted_iota(jnp.int32, (8, 1), 0)
    packed = unit_f[16:24, :] + jnp.where(rid == 6, q_own[...], 0.0)
    slope_out[...] = jnp.concatenate([packed[:, 0:half], packed[:, half:rows]], 0).astype(BF16)

    def slope_copy(k):
        slot = g * 4 + k
        return remote(slope_out, slope_in.at[slot], sem_slope_s.at[k], sem_slope_r.at[slot], dev(1, lax.rem(e + k, 4)))

    @pl.when(targetd)
    def _():
        slope_copy(0).start()

    for k in range(1, 4):
        slope_copy(k).start()

    ones = (lax.broadcasted_iota(jnp.int32, (16, rows), 0) == 0).astype(BF16)
    h1x[HID : HID + 16, :] = ones
    h2x[HID : HID + 16, :] = ones

    def curves(u):
        h, t = silu_half(u)
        c = 1.0 + t
        d = 1.0 - t
        return h, c + h * d, (c * d) * (1.0 - u * t)

    def body_a(i, _):
        sl = pl.ds(pl.multiple_of(i * BLOCK, BLOCK), BLOCK)
        h, a1, q1 = curves(dot(w1[...], x_b[:, sl]))
        hb = h.astype(BF16)
        h1x[0:HID, sl] = hb
        s1[:, sl] = a1.astype(BF16)
        h, a2, q2 = curves(halves(dot(f0[...], hb)) + vec[:, 0:1])
        hb = h.astype(BF16)
        h2x[0:HID, sl] = hb
        s2[:, sl] = a2.astype(BF16)
        h, a3, q3 = curves(halves(dot(f1[...], hb)) + vec[:, 1:2])
        hb = h.astype(BF16)
        h3s[:, sl] = hb
        s3[:, sl] = a3.astype(BF16)
        r = dot(eq[...], hb)
        value[:, sl] = r[0:1] + r[1:2] + vec[0:1, 8:9]
        last = vec[:, 2:3]
        db = (last * a3).astype(BF16)
        d3s[:, sl] = db
        k3[:, sl] = (last * q3).astype(BF16)
        m = halves(dot(b1[...], db))
        db = (m * a2).astype(BF16)
        d2s[:, sl] = db
        k2[:, sl] = (m * q2).astype(BF16)
        m = halves(dot(b0[...], db))
        db = (m * a1).astype(BF16)
        d1s[:, sl] = db
        k1[:, sl] = (m * q1).astype(BF16)
        slope = halves(dot(ga[...], db))
        inv = lax.rsqrt(jnp.sum(slope * slope, axis=0, keepdims=True) + 0.01)
        unit_f[0:8, sl] = slope * inv
        unit_f[8:9, sl] = inv
        return 0

    lax.fori_loop(0, blocks, body_a, 0)
    unit_out[...] = jnp.concatenate([unit_f[0:8, 0:half], unit_f[0:8, half:rows]], 0).astype(BF16)

    def unit_copy(k):
        p = lax.rem(me + k, 8)
        return remote(unit_out, unit_in.at[k - 1], sem_unit_s.at[k - 1], sem_unit_r.at[k - 1], dev(p // 4, lax.rem(p, 4)))

    for k in range(1, 8):
        unit_copy(k).start()

    class Exchange:
        def __init__(self, index, part, into, inbox, base, count, wide):
            self.index, self.part, self.into, self.inbox, self.base, self.count, self.wide = index, part, into, inbox, base, count, wide
            self.each = count // (n_dp * (4 if wide else 1))

        def rows_of(self, shard):
            first = self.base + (e * n_dp + shard if self.wide else shard) * self.each
            return pl.ds(pl.multiple_of(first, 8), self.each)

        def scatter(self, k):
            to = lax.rem(z + k, n_dp)
            return remote(
                self.part.at[self.rows_of(to)], self.inbox.at[k - 1], rs_s.at[self.index, k - 1], rs_r.at[self.index, k - 1], {"dp": to}
            )

        def gather(self, k):
            mine = self.into.at[self.rows_of(z)]
            return remote(mine, mine, ag_s.at[self.index, k - 1], ag_r.at[self.index, k - 1], {"dp": lax.rem(z + k, n_dp)})

        def across(self, k):
            there = self.into.at[self.rows_of(lax.rem(z + n_dp - k, n_dp))]
            return remote(there, there, xf_s.at[self.index, k], xf_r.at[self.index, k], dev(1 - g, e))

        def start(self):
            for k in range(1, n_dp):
                self.scatter(k).start()

        def reduce(self):
            total = self.part[self.rows_of(z), :]
            for k in range(1, n_dp):
                self.scatter(k).wait_recv()
                total = total + self.inbox[k - 1]
            self.into[self.rows_of(z), :] = total
            for k in range(1, n_dp):
                self.gather(k).start()
            self.across(0).start()

        def forward(self):
            for k in range(1, n_dp):
                self.gather(k).wait_recv()
                self.across(k).start()

        def sent(self):
            for k in range(1, n_dp):
                self.scatter(k).wait_send()
                self.gather(k).wait_send()
            for k in range(n_dp):
                self.across(k).wait_send()

        def arrived(self):
            for k in range(n_dp):
                self.across(k).wait_recv()

    small_c = part_c.shape[0] - 2 * HID
    ex_h1 = Exchange(0, part_c, sum_c.at[g], in_h1, HID, HID, False)
    ex_h0 = Exchange(1, part_c, sum_c.at[g], in_h0, 0, HID, False)
    ex_sm = Exchange(2, part_c, sum_c.at[g], in_sm, 2 * HID, small_c, False)
    ex_ac = Exchange(3, part_a, sum_a, in_ac, 0, part_a.shape[0], True)
    quarter = part_a.shape[0] // 4

    def spread_actor(k):
        mine = sum_a.at[pl.ds(pl.multiple_of(e * quarter, 8), quarter)]
        return remote(mine, mine, ef_s.at[k - 1], ef_r.at[k - 1], dev(g, lax.rem(e + k, 4)))

    lane = lax.broadcasted_iota(jnp.int32, (1, HID), 1)
    rid32 = lax.broadcasted_iota(jnp.int32, (32, 1), 0)

    @pl.when(online)
    def _():
        total = slope_out[...].astype(F32)
        for k in (0, 1, 2, 3, 5, 6, 7):
            remote(slope_out, slope_in.at[k], sem_slope_s.at[0], sem_slope_r.at[k], dev(1, e)).wait_recv()
            total = total + slope_in[k].astype(F32)
        total = jnp.concatenate([total[0:8], total[8:16]], 1) * (1.0 / critics)
        d_sample = -valid * total
        d_logp = ALPHA * valid
        sample = pi_act[...]
        th = heads[0:8, :]
        spread_e = heads[8:16, :]
        dz = (d_sample * (1.0 - sample * sample) + d_logp * 2.0 * sample) * ok8
        dls = (dz * spread_e - d_logp) * (3.5 * (1.0 - th * th)) * ok8
        heads[24:40, :] = jnp.zeros((16, rows), F32)
        heads[24:30, :] = dz[0:ACT]
        heads[30:36, :] = dls[0:ACT]
        actor_sum = jnp.sum(valid * (ALPHA * heads[16:17, :] - total[6:7]), axis=1, keepdims=True)
        count = jnp.sum(valid, axis=1, keepdims=True)
        for acc in (acc_h1, acc_h0, acc_x, acc_o):
            acc[...] = jnp.zeros_like(acc)
        one16 = (lax.broadcasted_iota(jnp.int32, (16, BLOCK), 0) == 0).astype(BF16)

        def body_c(i, _):
            sl = pl.ds(pl.multiple_of(i * BLOCK, BLOCK), BLOCK)
            kept = actor_layers(x_b[:, sl])
            slopes = [(1.0 + t) + h * (1.0 - t) for _, h, t in kept]
            do = heads[24:40, sl].astype(BF16)
            acc_o[0:16, :] += dot_t(do, kept[2][0])
            d3 = (dot(aot[...], jnp.concatenate([do, do], 0)) * (0.5 * slopes[2])).astype(BF16)
            acc_h1[...] += dot_t(jnp.concatenate([kept[1][0], one16], 0), d3)
            d2 = (halves(dot(ab1[...], d3)) * slopes[1]).astype(BF16)
            acc_h0[...] += dot_t(jnp.concatenate([kept[0][0], one16], 0), d2)
            d1 = (halves(dot(ab0[...], d2)) * slopes[0]).astype(BF16)
            acc_x[...] += dot_t(x_b[0:32, sl], d1)
            acc_o[16:32, 0:128] += dot_t(one16, jnp.concatenate([do, jnp.zeros((112, BLOCK), BF16)], 0))
            return 0

        lax.fori_loop(0, blocks, body_c, 0)
        part_a[0:HID, :] = acc_h0[0:HID, :]
        part_a[HID : 2 * HID, :] = acc_h1[0:HID, :]
        stats = jnp.where(lane == 0, actor_sum, jnp.where(lane == 1, count, 0.0))
        small = acc_x[...]
        small = small + jnp.where(rid32 == 18, acc_h0[HID : HID + 1, :], 0.0)
        small = small + jnp.where(rid32 == 19, acc_h1[HID : HID + 1, :], 0.0)
        small = small + jnp.where(rid32 == 20, acc_o[16:17, :], 0.0)
        small = small + jnp.where(rid32 == 21, stats, 0.0)
        part_a[2 * HID : 2 * HID + 32, :] = small
        part_a[2 * HID + 32 : 2 * HID + 48, :] = acc_o[0:16, :]
        rest = part_a.shape[0] - 2 * HID - 48
        part_a[2 * HID + 48 :, :] = jnp.zeros((rest, HID), F32)
        ex_ac.start()

    @pl.when(targetd)
    def _():
        least_in[0] = least[...]
        for k in range(1, 4):
            least_target(k).wait_recv()

    @pl.when(online)
    def _():
        for k in range(4):
            least_online(k).wait_recv()

    low = jnp.minimum(jnp.minimum(least_in[0], least_in[1]), jnp.minimum(least_in[2], least_in[3]))
    target[...] = rewards[...] + GAMMA * (1.0 - done[...].astype(F32)) * low

    spread = unit_out[...].astype(F32)
    for k in range(1, 8):
        unit_copy(k).wait_recv()
        spread = spread + unit_in[k - 1].astype(F32)
    spread = jnp.concatenate([spread[0:8], spread[8:16]], 1)
    unit = unit_f[0:8, :]
    inv = unit_f[8:9, :]
    d_unit = (2.0 * ETA / (critics - 1)) * valid * (spread - unit)
    along = jnp.sum(d_unit * unit, axis=0, keepdims=True)
    dg = (d_unit - unit * along) * inv
    gap = value[...] - target[...]
    dv = 2.0 * valid * gap
    diverse = jnp.sum(valid * jnp.sum(unit * (spread - unit), axis=0, keepdims=True), axis=1, keepdims=True)
    errors = jnp.sum(valid * gap * gap, axis=1, keepdims=True)
    dv_sum = jnp.sum(dv, axis=1, keepdims=True)
    dgb = dg.astype(BF16)
    dg_b[...] = jnp.concatenate([dgb, dgb], 0)
    rid16 = lax.broadcasted_iota(jnp.int32, (16, 1), 0)
    dv_b[...] = jnp.where(rid16 == 0, dv, jnp.where(rid16 == 1, 1.0, 0.0)).astype(BF16)

    for acc in (acc_h1, acc_h1t, acc_h0, acc_h0t, acc_x, acc_t, acc_last):
        acc[...] = jnp.zeros_like(acc)

    def body_b1(i, _):
        sl = pl.ds(pl.multiple_of(i * BLOCK, BLOCK), BLOCK)
        rows_dv = dv_b[:, sl]
        dvh = (rows_dv[0:1].astype(F32) * 0.5).astype(BF16)
        tp = dot(t1w[...], dg_b[:, sl]).astype(BF16)
        k1[:, sl] = k1[:, sl] * tp
        th1 = s1[:, sl] * tp
        tp = halves(dot(f0[...], th1)).astype(BF16)
        k2[:, sl] = k2[:, sl] * tp
        th2 = s2[:, sl] * tp
        tp = halves(dot(f1[...], th2)).astype(BF16)
        th3 = s3[:, sl] * tp
        d3 = d3s[:, sl]
        ap3 = dvh * d3 + k3[:, sl] * tp
        k3[:, sl] = ap3
        last = dot_t(rows_dv, h3s[:, sl])
        lone = dot_t(rows_dv, th3)
        acc_last[...] += last[0:8] + jnp.where(rid == 0, lone[1:2], 0.0)
        h3s[:, sl] = th1
        acc_h1[...] += dot_t(h2x[:, sl], ap3)
        acc_h1t[...] += dot_t(th2, d3)
        return 0

    def body_b2(i, _):
        sl = pl.ds(pl.multiple_of(i * BLOCK, BLOCK), BLOCK)
        ah = halves(dot(b1[...], k3[:, sl])).astype(BF16)
        ap2 = s2[:, sl] * ah + k2[:, sl]
        k2[:, sl] = ap2
        acc_h0[...] += dot_t(h1x[:, sl], ap2)
        acc_h0t[...] += dot_t(h3s[:, sl], d2s[:, sl])
        return 0

    def body_b3(i, _):
        sl = pl.ds(pl.multiple_of(i * BLOCK, BLOCK), BLOCK)
        ah = halves(dot(b0[...], k2[:, sl])).astype(BF16)
        ap1 = s1[:, sl] * ah + k1[:, sl]
        acc_x[...] += dot_t(x_b[0:32, sl], ap1)
        acc_t[...] += dot_t(dg_b[:, sl], d1s[:, sl])
        return 0

    lax.fori_loop(0, blocks, body_b1, 0)
    part_c[HID : 2 * HID, :] = acc_h1[0:HID, :] + 0.5 * acc_h1t[...]
    ex_h1.start()

    @pl.when(online)
    def _():
        ex_ac.reduce()

    lax.fori_loop(0, blocks, body_b2, 0)
    part_c[0:HID, :] = acc_h0[0:HID, :] + 0.5 * acc_h0t[...]
    ex_h0.start()
    ex_h1.reduce()

    @pl.when(online)
    def _():
        ex_ac.forward()
        for k in range(1, 4):
            spread_actor(k).start()

    lax.fori_loop(0, blocks, body_b3, 0)
    stats = jnp.where(lane == 0, errors, jnp.where(lane == 1, diverse, 0.0))
    small = acc_x[...]
    small = small + jnp.where(rid32 == 18, acc_h0[HID : HID + 1, :], 0.0)
    small = small + jnp.where(rid32 == 19, acc_h1[HID : HID + 1, :], 0.0)
    small = small + jnp.where(rid32 == 20, stats, 0.0)
    small = small + jnp.where(rid32 == 22, jnp.where(lane == 0, dv_sum, 0.0), 0.0)
    small = small + jnp.where(rid32 == 23, acc_last[0:1, :], 0.0)
    part_c[2 * HID : 2 * HID + 24, :] = small[0:24]
    part_c[2 * HID + 24 : 2 * HID + 32, :] = small[24:32] + 0.5 * acc_t[0:8, :]
    if small_c > 32:
        part_c[2 * HID + 32 :, :] = jnp.zeros((small_c - 32, HID), F32)
    ex_sm.start()
    ex_h1.forward()
    ex_h0.reduce()
    ex_sm.reduce()

    @pl.when(targetd)
    def _():
        ex_ac.arrived()
        for k in range(1, 4):
            spread_actor(k).start()

    ex_h0.forward()
    ex_sm.forward()

    def local(src, dst, k):
        return pltpu.make_async_copy(src, dst, sem_out.at[k])

    @pl.when(online)
    def _():
        for copy in (local(c_edge, out_pe, 0), local(c_hidden, out_ph, 1), local(c_bias, out_pb, 2)):
            copy.start()
            copy.wait()

    @pl.when(targetd)
    def _():
        for what in range(4):
            param_copy(0, what).wait_recv()
        for copy in (local(p_edge, out_pe, 0), local(p_hidden, out_ph, 1), local(p_bias, out_pb, 2)):
            copy.start()
            copy.wait()

    for k in range(1, 4):
        spread_actor(k).wait_recv()
    copy_a = local(sum_a, out_a, 3)
    copy_a.start()
    for ex in (ex_h1, ex_h0, ex_sm):
        ex.arrived()
    copy_c = local(sum_c, out_c, 4)
    copy_c.start()

    @pl.when(online)
    def _():
        for m in range(2):
            for what in range(4):
                param_copy(m, what).wait_send()
        remote(pi_act, pi_act, sem_pi_s, sem_pi_r, dev(0, e)).wait_send()
        ex_ac.sent()

    @pl.when(targetd)
    def _():
        for k in range(1, 4):
            least_target(k).wait_send()
        for k in range(4):
            least_online(k).wait_send()
        slope_copy(0).wait_send()

    for k in range(1, 4):
        slope_copy(k).wait_send()
        spread_actor(k).wait_send()
    for k in range(1, 8):
        unit_copy(k).wait_send()
    for ex in (ex_h1, ex_h0, ex_sm):
        ex.sent()
    copy_a.wait()
    copy_c.wait()


def sizes(n_dp):
    return 2 * HID + up(CRITIC_SMALL, 8 * n_dp), up(2 * HID + ACTOR_SMALL, 32 * n_dp)


def fused(n_dp, rows, data, own, aparams):
    v = pltpu.VMEM
    big = lambda n=HID: v((n, rows), BF16)
    dma = pltpu.SemaphoreType.DMA
    size_c, size_a = sizes(n_dp)
    scratch = [
        v((32, rows), F32), v((32, rows), F32), v((8, rows), F32),
        v((64, rows), BF16), v((64, rows), BF16), v((8, rows), F32),
        v((128, HID), F32), v((HID, 128), F32), v((2, HID, 128), F32), v((HID, 128), F32),
        v((2, 24, HID), F32), v((2, 2, HID, HID), F32), v((2, 4, HID), F32),
        v((HID, 64), BF16), v((512, HID), BF16), v((512, HID), BF16), v((512, HID), BF16), v((512, HID), BF16),
        v((16, HID), BF16), v((HID, 16), BF16), v((16, HID), BF16),
        v((2, HID, 64), BF16), v((2, 512, HID), BF16), v((2, 512, HID), BF16), v((2, 16, HID), BF16),
        v((HID, 64), BF16), v((512, HID), BF16), v((512, HID), BF16), v((512, HID), BF16), v((512, HID), BF16),
        v((32, HID), BF16), v((HID, 32), BF16),
        big(272), big(272), big(), big(), big(), big(), big(), big(), big(), big(), big(), big(),
        v((40, rows), F32),
        v((1, rows), F32), v((24, rows), F32), v((16, rows // 2), BF16), v((7, 16, rows // 2), BF16),
        v((16, rows), BF16), v((16, rows), BF16),
        v((16, rows // 2), BF16), v((8, 16, rows // 2), BF16), v((1, rows), F32),
        v((1, rows), F32), v((4, 1, rows), F32), v((1, rows), F32),
        v((272, HID), F32), v((HID, HID), F32), v((272, HID), F32), v((HID, HID), F32),
        v((32, HID), F32), v((16, HID), F32), v((8, HID), F32), v((32, HID), F32),
        v((size_c, HID), F32), v((size_a, HID), F32), v((2, size_c, HID), F32), v((size_a, HID), F32),
        v((n_dp - 1, HID // n_dp, HID), F32), v((n_dp - 1, HID // n_dp, HID), F32),
        v((n_dp - 1, (size_c - 2 * HID) // n_dp, HID), F32), v((n_dp - 1, size_a // (4 * n_dp), HID), F32),
        dma((2, 4)), dma((2, 4)), dma, dma, dma((8,)), dma((4,)), dma((7,)), dma((7,)), dma((4,)), dma((8,)),
        dma((4, n_dp - 1)), dma((4, n_dp - 1)), dma((4, n_dp - 1)), dma((4, n_dp - 1)), dma((4, n_dp)), dma((4, n_dp)),
        dma((3,)), dma((3,)), dma((5,)),
    ]
    spec = pl.BlockSpec(memory_space=pltpu.VMEM)
    anyspace = pl.BlockSpec(memory_space=pl.ANY)
    shape = lambda *s: jax.ShapeDtypeStruct(s, F32)
    return pl.pallas_call(
        functools.partial(kernel, n_dp, rows, False),
        out_shape=(
            shape(2, size_c, HID), shape(size_a, HID), shape(2, 24, HID), shape(2, 2, HID, HID), shape(2, 4, HID),
        ),
        in_specs=[spec] * 5 + [pl.BlockSpec(memory_space=pltpu.SMEM)] + [spec] * 6,
        out_specs=(anyspace,) * 5,
        scratch_shapes=scratch,
        compiler_params=pltpu.CompilerParams(collective_id=0, has_side_effects=True, vmem_limit_bytes=63 * 2**20),
        name="edac_gradients",
    )(*data, *own, *aparams)


def adamw(param, grad, first, second):
    first_new = BETA_ONE * first + (1.0 - BETA_ONE) * grad
    second_new = BETA_TWO * second + (1.0 - BETA_TWO) * grad * grad
    ratio = first_new / (1.0 - BETA_ONE**STEP) / (jnp.sqrt(second_new / (1.0 - BETA_TWO**STEP)) + EPS)
    return (param - LEARN * (ratio + DECAY * param), first_new, second_new)


def update_kernel(
    gh, gs, gah, gas,
    own_e, own_h, own_b, on_e, on_h, on_b, em, ev, hm, hv, bm, bv,
    ae, ah, ab, aem, aev, ahm, ahv, abm, abv,
    o_e, o_h, o_b, o_em, o_ev, o_hm, o_hv, o_bm, o_bv,
    o_ae, o_ah, o_ab, o_aem, o_aev, o_ahm, o_ahv, o_abm, o_abv, o_ms, o_as,
    ge, gb, gae, gab,
):
    online = lax.axis_index("grp") == 1
    scale = 1.0 / gas[21:22, 1:2]

    def critic(own, param, grad, first, second):
        master, m_new, v_new = adamw(param, grad, first, second)
        polyak = TAU * master.astype(BF16).astype(F32) + (1.0 - TAU) * own
        return jnp.where(online, master, polyak), m_new, v_new

    o_h[0, 0], o_hm[0, 0], o_hv[0, 0] = critic(own_h[0, 0], on_h[0, 0], gh[0] * scale, hm[0, 0], hv[0, 0])
    o_ah[0], o_ahm[0], o_ahv[0] = adamw(ah[0], gah[...] * scale, ahm[0], ahv[0])

    @pl.when(pl.program_id(0) == 0)
    def _():
        for m in range(2):
            small = gs.at[1 - m]
            ge[0:OBS, :] = small[0:OBS, :]
            ge[OBS : OBS + ACT, :] = small[24 : 24 + ACT, :]
            ge[23:24, :] = small[23:24, :]
            gb[0:3, :] = small[17:20, :]
            gb[3:4, :] = small[22:23, :]
            o_e[m], o_em[m], o_ev[m] = critic(own_e[m], on_e[m], ge[...] * scale, em[m], ev[m])
            o_b[m], o_bm[m], o_bv[m] = critic(own_b[m], on_b[m], gb[...] * scale, bm[m], bv[m])
            o_ms[m : m + 1, :] = small[20:21, 0:2]
        gae[0:OBS, :] = gas[0:OBS, :]
        gae[OBS : OBS + 2 * ACT, :] = gas[32 : 32 + 2 * ACT, :]
        gab[0:3, :] = gas[17:20, :]
        gab[3:4, :] = gas[20:21, :]
        o_ae[...], o_aem[...], o_aev[...] = adamw(ae[...], gae[...] * scale, aem[...], aev[...])
        o_ab[...], o_abm[...], o_abv[...] = adamw(ab[...], gab[...] * scale, abm[...], abv[...])
        o_as[...] = gas[21:22, 0:2]


def update(grads, own, online, moments, aparams, amoments):
    size_c = grads[0].shape[1]
    shape = lambda *s: jax.ShapeDtypeStruct(s, F32)
    whole = lambda *s: pl.BlockSpec(s, lambda i: (0,) * len(s))
    mat = pl.BlockSpec((1, 1, HID, HID), lambda i: (i // 2, i % 2, 0, 0))
    amat = pl.BlockSpec((1, HID // 2, HID), lambda i: (i // 2, i % 2, 0))
    edge, bias, aedge, abias = whole(2, 24, HID), whole(2, 4, HID), whole(29, HID), whole(4, HID)
    in_specs = [
        pl.BlockSpec((1, HID, HID), lambda i: (1 - i // 2, i % 2, 0)),
        pl.BlockSpec((2, 32, HID), lambda i: (0, 16, 0)),
        pl.BlockSpec((HID // 2, HID), lambda i: (i, 0)),
        pl.BlockSpec((ACTOR_SMALL, HID), lambda i: (8, 0)),
        edge, mat, bias, edge, mat, bias, edge, edge, mat, mat, bias, bias,
        aedge, amat, abias, aedge, aedge, amat, amat, abias, abias,
    ]
    out_specs = (edge, mat, bias, edge, edge, mat, mat, bias, bias, aedge, amat, abias, aedge, aedge, amat, amat, abias, abias,
                 whole(2, 2), whole(1, 2))
    e_, h_, b_ = shape(2, 24, HID), shape(2, 2, HID, HID), shape(2, 4, HID)
    ae_, ah_, ab_ = shape(29, HID), shape(2, HID, HID), shape(4, HID)
    return pl.pallas_call(
        update_kernel,
        grid=(4,),
        out_shape=(e_, h_, b_, e_, e_, h_, h_, b_, b_, ae_, ah_, ab_, ae_, ae_, ah_, ah_, ab_, ab_, shape(2, 2), shape(1, 2)),
        in_specs=in_specs,
        out_specs=out_specs,
        scratch_shapes=[pltpu.VMEM((24, HID), F32), pltpu.VMEM((4, HID), F32), pltpu.VMEM((29, HID), F32), pltpu.VMEM((4, HID), F32)],
        name="adamw",
    )(grads[0], grads[0], grads[1], grads[1], *own, *online, *moments, *aparams, *amoments)


def body(
    n_dp,
    states, actions, rewards, done, noise, counts,
    crit_edge, crit_hidden, crit_bias, edge_m, edge_v, hidden_m, hidden_v, bias_m, bias_v,
    act_edge, act_hidden, act_bias, act_edge_m, act_edge_v, act_hidden_m, act_hidden_v, act_bias_m, act_bias_v,
):
    rows = states.shape[0]
    own = (crit_edge[0], crit_hidden[0], crit_bias[0])
    aparams = (act_edge, act_hidden, act_bias)
    data = (states.T, actions.T, noise.T, rewards[None], done[None], counts)
    grad_c, grad_a, on_e, on_h, on_b = fused(n_dp, rows, data, own, aparams)
    out = update(
        (grad_c, grad_a), own, (on_e, on_h, on_b),
        (edge_m, edge_v, hidden_m, hidden_v, bias_m, bias_v), aparams,
        (act_edge_m, act_edge_v, act_hidden_m, act_hidden_v, act_bias_m, act_bias_v),
    )
    return (*(o[None] for o in out[:3]), *out[3:19], out[19][0])


def solution(mesh):
    member = P("grp", "ens", None, None)
    hidden = P("grp", "ens", None, None, None)
    mom = P("ens", None, None)
    mom_h = P("ens", None, None, None)
    return jax.shard_map(
        functools.partial(body, mesh.shape["dp"]),
        mesh=mesh,
        in_specs=(
            P("dp", None), P("dp", None), P("dp"), P("dp"), P("dp", None), P("dp"),
            member, hidden, member, mom, mom, mom_h, mom_h, mom, mom,
        ) + (P(),) * 9,
        out_specs=(member, hidden, member, mom, mom, mom_h, mom_h, mom, mom) + (P(),) * 9 + (P("ens", None), P()),
        check_vma=False,
    )
```

time: 211 us -> 109 us (0.52)
  waiting for transfers between devices: 113 us -> 0 us
  Pallas kernels: 48.2 us -> 108 us
  local copies, waits for them, and re-layouts: 19.6 us -> 0 us
  between operations: 15.5 us -> 1.47 us
  other arithmetic: 10 us -> 0 us
  starting transfers between devices: 4.13 us -> 0 us
    psum x2 -> x0, waiting for transfers between devices: 101 us -> none  [the longest x1 62.3 us: body(): grad_c, grad_a = lax.psum((grad_c, grad_a), 'dp')]
    pallas_call x1 -> x2, Pallas kernels: 48.2 us -> 108 us  [the longest x1 100 us: fused(): pl.pallas_call(functools.partial(kernel, n_dp, rows, False), out_shape=(s...]
    all_gather x1 -> x0, waiting for transfers between devices: 12.2 us -> none  [body(): both = lax.all_gather(grad_c, 'grp')[::-1]]
    concatenate x1 -> x0, local copies, waits for them, and re-layouts: 8.73 us -> none  [body(): jnp.concatenate([states_t[:OBS], one, zero(6), states_t[OBS:], one, zero(...]
    slice x20 -> x0, local copies, waits for them, and re-layouts: 7.52 us -> none  [the longest x1 1.26 us: body(): total = grad_a[2 * HID + 21, 1]]
    broadcast_in_dim x3 -> x0, other arithmetic: 5.3 us -> none  [body(): outs.append(jnp.where(online, master, polyak)[None])]
    ppermute x3 -> x0, starting transfers between devices: 4.01 us -> none  [body(): onl = [lax.ppermute(p, 'grp', [(1, 0)]) for p in own]]
    sub x3 -> x0, other arithmetic: 2.69 us -> none  [adamw(): return (param - LEARN * (ratio + DECAY * param), first_new, second_new)]
  transfers between devices with their start and end apart: 6 -> 0, of which waited for: 3 -> 0; matrix products, arithmetic and copies ran while one was open for 7% -> 0% of each run, Pallas kernels for 0% -> 0%
where the time goes in v2:
time: 109 us
  Pallas kernels  108 us (99%)
  between operations  1.47 us (1%)
    pallas_call x1, Pallas kernels, fused(): pl.pallas_call(functools.partial(kernel, n_dp, rows, False), out_shape=(s...  100 us
    pallas_call x1, Pallas kernels, update(): pl.pallas_call(update_kernel, grid=(4,), out_shape=(e_, h_, b_, e_, e_, h...  7.31 us

profile of v2, /device:TPU:0, one launch (start us, length us, event | category | flops | bytes accessed | tf_op | source)
XLA Modules:
  0.0 109.0 jit_solution(221712645853481104)
XLA Ops:
  1.3 100.2 %edac_gradients.1 = (f32[2,544,256]{2,1,0:T(8,128)}, f32[640,256]{1,0:T(8,128)}, f32[2,24,256]{2,1,0:T(8,128)}, f32[2,2,256,256]{3,2,1,0:T(8,128)}, f32[2,4,256]{2,1,0:T(4,128)}) custom-call(f32[34,4096]{1,0:T(8,128)} %bitcast.14, f32[6,4096]{1,0:T(8,128)} %bitcast.18, f32[12,4096]{1,0:T(8,128)} %bitcast.15, f32[1,4096]{1,0:T(1,128)} %bitcast.21, ...), custom_call_target="tpu_custom_call" | custom-call | tf_op jit(solution)/shard_map/edac_gradients/pallas_call | solution.py:723
  101.6 7.3 %adamw.1 = (f32[2,24,256]{2,1,0:T(8,128)}, f32[2,2,256,256]{3,2,1,0:T(8,128)}, f32[2,4,256]{2,1,0:T(4,128)}, f32[2,24,256]{2,1,0:T(8,128)}, f32[2,24,256]{2,1,0:...) custom-call(f32[2,544,256]{2,1,0:T(8,128)} %get-tuple-element.45.gh., ...), custom_call_target="tpu_custom_call" | custom-call | tf_op jit(solution)/shard_map/adamw/pallas_call | solution.py:802
